TPU v7x, 128 devices: a whole 4x4x4 slice. The times are simulated.
128 devices in a mesh: replica: 8 (over x, y_lo), tensor: 16 (over y_hi, z, core).
Axes of the slice: x: 4, y: 4 (y_hi: 2, y_lo: 2; y = y_hi * 2 + y_lo), z: 4, core: 2. Of those that a mesh axis runs over, the one named last changes fastest.
Arguments:
- tokens: bfloat16 [8192, 8192], P(('replica', 'tensor')), may hold values from -16 to 16
- norm_gain: float32 [8192], replicated, may hold values from 0.5 to 1.5
- query_weight: bfloat16 [8192, 8192], P(None, 'tensor'), may hold values from -0.5 to 0.5
- kv_weight: bfloat16 [8192, 2048], P(None, 'tensor'), may hold values from -0.5 to 0.5
- out_weight: bfloat16 [8192, 8192], P('tensor'), may hold values from -0.5 to 0.5
- pseudo_grad: bfloat16 [8, 8192, 1024], P('replica', 'tensor'), may hold values from -6 to 6
- grad_exps: int32 [8, 8192, 8], P('replica', 'tensor'), may hold values from -2 to 1
- params: bfloat16 [8192, 1024], P('tensor'), may hold values from -4 to 4
- momentum: float32 [8192, 1024], P('tensor', 'replica'), may hold values from -4 to 4
Outputs:
- attended: bfloat16 [8192, 8192], P(('replica', 'tensor'))
- new_params: bfloat16 [8192, 1024], P('tensor')
- new_momentum: float32 [8192, 1024], P('tensor', 'replica')
All inputs are finite; a program needn't handle non-finite values. Where the computation divides by a largest or mean magnitude, that divisor is 1e-20 or more.
Results may differ from a plain program's by a relative error of at most 0.019.
Values may be sent and summed in bfloat16 or wider, within the bound.
No kernel may reach another device: no remote copies, remote signals or barrier semaphores. Data moves between devices by JAX's collectives and lax.ppermute only.
A program may use at most 128 MiB of HBM per device.

v0:
```python
import math

import jax
import jax.numpy as jnp
from jax import lax
from jax.sharding import PartitionSpec as P

HEAD_DIM = 128
HBLOCK = 128


def partner(block, axis, apart):
    count = lax.axis_size(axis)
    route = []
    for low in range(count):
        high = low | 1 << apart
        if high != low and high < count:
            route += [(low, high), (high, low)]
    return lax.ppermute(block, axis, route)


def hadamard_table(width):
    index = jnp.arange(width, dtype=jnp.int32)
    common = jnp.bitwise_and(index[:, None], index[None, :])
    parity = jnp.zeros((width, width), jnp.int32)
    for bit in range(int(math.log2(width))):
        parity = parity + jnp.bitwise_and(jnp.right_shift(common, bit), 1)
    sign = 1.0 - 2.0 * jnp.bitwise_and(parity, 1).astype(jnp.float32)
    return sign / math.sqrt(width)


def rotate(values, table):
    shaped = values.reshape(-1, table.shape[0])
    return jnp.dot(shaped, table, precision=lax.Precision.HIGHEST).reshape(values.shape)


def dequantize(codes, exps, width):
    shape = codes.shape
    blocks = codes.reshape(shape[:-1] + (shape[-1] // width, width)).astype(jnp.float32)
    return (blocks * jnp.exp2(exps.astype(jnp.float32))[..., None]).reshape(shape)


def normalize(rows, gain):
    values = rows.astype(jnp.float32)
    power = jnp.mean(values * values, axis=-1, keepdims=True)
    return (values * lax.rsqrt(power + 1e-05) * gain).astype(jnp.bfloat16)


def attend(query, keys, values):
    count = keys.shape[0]
    scores = jnp.einsum("thd,sd->hts", query, keys, preferred_element_type=jnp.float32) * (
        1.0 / math.sqrt(keys.shape[1])
    )
    causal = jnp.arange(count)[:, None] >= jnp.arange(count)[None, :]
    scores = jnp.where(causal[None], scores, -jnp.inf)
    peak = jnp.max(scores, axis=-1, keepdims=True)
    expo = jnp.exp(scores - peak)
    probs = (expo / jnp.sum(expo, axis=-1, keepdims=True)).astype(jnp.bfloat16)
    mixed = jnp.einsum("hts,sd->thd", probs, values, preferred_element_type=jnp.float32)
    return mixed.astype(jnp.bfloat16).reshape(count, -1)


def local(
    tokens, norm_gain, query_weight, kv_weight, out_weight, pseudo_grad, grad_exps, params, momentum
):
    width = HBLOCK
    table = hadamard_table(width)
    replicas = lax.axis_size("replica")
    terms = dequantize(pseudo_grad[0], grad_exps[0], width)
    summed = lax.psum_scatter(
        terms.astype(jnp.bfloat16), "replica", scatter_dimension=1, tiled=True
    ).astype(jnp.float32)
    averaged = rotate(summed / replicas, table)
    new_momentum = 0.9 * momentum + averaged
    update = 0.7 * (averaged + 0.9 * new_momentum)
    turned = rotate(update, table)
    row_count, col_count = turned.shape
    turned_blocks = turned.reshape(row_count, col_count // width, width)
    scales = (jnp.max(jnp.abs(turned_blocks), axis=-1) + 1e-06).astype(jnp.bfloat16)
    codes_out = (
        (turned_blocks / scales.astype(jnp.float32)[..., None])
        .astype(jnp.bfloat16)
        .reshape(row_count, col_count)
    )
    all_codes, all_scales = (
        lax.all_gather(codes_out, "replica", axis=1, tiled=True),
        lax.all_gather(scales, "replica", axis=1, tiled=True),
    )
    full_cols = all_codes.shape[1]
    rebuilt_blocks = (
        all_codes.reshape(row_count, full_cols // width, width).astype(jnp.float32)
        * all_scales.astype(jnp.float32)[..., None]
    )
    rebuilt = rotate(rebuilt_blocks.reshape(row_count, full_cols), table)
    new_params = (params.astype(jnp.float32) - rebuilt).astype(jnp.bfloat16)
    qcols = query_weight.shape[1]
    parity = lax.axis_index("tensor") % 2
    partner_cols = partner(kv_weight, "tensor", 0)
    combined = jnp.concatenate([query_weight, kv_weight, partner_cols], axis=1)
    projected = jnp.dot(
        normalize(lax.all_gather(tokens, "tensor", axis=0, tiled=True), norm_gain),
        combined,
        preferred_element_type=jnp.float32,
    )
    seq_len = projected.shape[0]
    query = projected[:, :qcols].astype(jnp.bfloat16).reshape(seq_len, qcols // HEAD_DIM, HEAD_DIM)
    mine = projected[:, qcols : qcols + HEAD_DIM].astype(jnp.bfloat16)
    theirs = projected[:, qcols + HEAD_DIM :].astype(jnp.bfloat16)
    keys = jnp.where(parity == 0, mine, theirs)
    values = jnp.where(parity == 0, theirs, mine)
    mixed = attend(query, keys, values)
    attended = lax.psum_scatter(
        jnp.dot(mixed, out_weight, preferred_element_type=jnp.float32).astype(jnp.bfloat16),
        "tensor",
        scatter_dimension=0,
        tiled=True,
    )
    return (attended, new_params, new_momentum)


def solution(mesh):
    return jax.shard_map(
        local,
        mesh=mesh,
        in_specs=(
            P(("replica", "tensor"), None),
            P(),
            P(None, "tensor"),
            P(None, "tensor"),
            P("tensor", None),
            P("replica", "tensor", None),
            P("replica", "tensor", None),
            P("tensor", None),
            P("tensor", "replica"),
        ),
        out_specs=(P(("replica", "tensor"), None), P("tensor", None), P("tensor", "replica")),
        check_vma=False,
    )
```

profile of v0, /device:TPU:0, one launch (start us, length us, event | category | flops | bytes accessed | tf_op | source)
XLA Modules:
  0.0 345.6 jit_solution(1699939151603711021)
XLA Ops:
  8.0 0.0 copy-start.4
  8.0 0.0 reduce-scatter.7.cloned.1.call-start
  8.1 0.8 exponential_bitcast_fusion
  8.8 0.1 copy.30
  8.9 0.6 mul.82
  9.6 1.8 fusion.18
  11.4 1.3 copy.37
  12.7 0.0 reduce-scatter.7.cloned.1.call-update
  12.7 0.0 all-gather.4.cloned.1.call-start
  12.8 0.5 all-gather.4.cloned.1.call-update
  13.3 0.0 all-gather.6.cloned.1.call-start
  13.3 0.1 collective-permute-start
  13.4 0.3 iota_compare_fusion
  13.8 51.7 %reduce-scatter.7.cloned.1.call-done = bf16[128,512]{1,0:T(8,128)(2,1)} async-done(((bf16[1024,512]{1,0:T(8,128)(2,1)}), bf16[128,512]{1,0:T(8,128)(2,1)}) %reduce-scatter.7.cloned.1.call-update) | async-done | bytes 131088
  65.5 1.1 copy.38
  66.6 0.0 copy-done.4
  66.6 0.4 multiply_add_fusion
  67.0 0.0 copy-start.1
  67.0 0.5 abs_reduce_fusion
  67.6 0.7 divide_convert_fusion.4
  68.2 0.0 copy-start.5
  68.2 0.0 all-gather.6.cloned.1.call-update
  68.3 0.2 reduce-scatter.5.cloned.1.call-start
  68.5 62.3 %all-gather.4.cloned.1.call-done = bf16[1024,8192]{1,0:T(8,128)(2,1)} async-done(((bf16[64,8192]{1,0:T(8,128)(2,1)}), bf16[1024,8192]{1,0:T(8,128)(2,1)}) %all-gather.4.cloned.1.call-update) | async-done | bytes 16777232 | tf_op jit(solution)/shard_map/all_gather | solution.py:101
  130.8 0.0 copy-start
  130.8 7.5 %fusion.1 = f32[1024]{0:T(1024)S(1)} fusion(bf16[1024,8192]{1,0:T(8,128)(2,1)} %all-gather.4.cloned.1.call-done), kind=kLoop, calls=%fused_computation.3 | loop fusion | flops 25164800 | bytes 16781312 | tf_op jit(solution)/shard_map/reduce_sum | solution.py:45
  138.2 0.0 copy-done.1
  138.3 0.0 collective-permute-done
  138.3 0.0 copy-done.5
  138.3 3.2 copy-done
  141.5 17.3 %fusion.23 = bf16[1024,768]{0,1:T(8,128)(2,1)S(1)} fusion(bf16[8192,128]{1,0:T(8,128)(2,1)} %collective-permute-done, bf16[8192,128]{1,0:T(8,128)(2,1)} %param.12, bf16[8192,512]{1,0:T(8,128)(2,1)} %param.11, bf16[1024,8192]{1,0:T(8,128)(2,1)S(1)} %copy-done, f32[8192]{0:T(1024)S(1)} %copy-done.5, f32[1024]{0:T(1024)S(1)} %add_rsqrt_fusion), kind=kOutput, calls=%fused_computation.30 | convolution fusion | flops 12956991488 | bytes 30969856 | tf_op jit(solution)/shard_map/dot_general | solution.py:100
  158.7 0.0 copy-start.3
  158.7 1.2 copy-done.3
  159.9 0.1 slice.17
  160.0 10.6 %fusion.89 = (f32[4,1024]{1,0:T(4,128)S(1)}, f32[4,1024,1024]{1,2,0:T(8,128)}) fusion(pred[1024,1024]{0,1:T(8,128)(4,1)S(1)} %iota_compare_fusion, bf16[1024,4,128]{0,2,1:T(8,128)(2,1)S(1)} %bitcast.53, pred[]{:T(512)S(6)} %eq.6, bf16[1024,768]{0,1:T(8,128)(2,1)} %copy-done.3), kind=kOutput, calls=%fused_computation.96 | convolution fusion | flops 1090651136 | bytes 19415040 | tf_op jit(solution)/shard_map/sub | solution.py:57
  170.6 7.3 %fusion.28 = bf16[128,4,1024]{2,0,1:T(8,128)(2,1)S(1)} fusion(f32[4,1024,1024]{1,2,0:T(8,128)} %get-tuple-element.6, f32[4,1024]{1,0:T(4,128)S(1)} %get-tuple-element.5, pred[]{:T(512)S(6)} %eq.6, bf16[1024,768]{0,1:T(8,128)(2,1)} %copy-done.3), kind=kOutput, calls=%fused_computation.31 | convolution fusion | flops 1082785792 | bytes 18366464 | tf_op jit(solution)/shard_map/hts,sd->thd/dot_general | solution.py:59
  177.8 16.0 %convolution_convert_fusion = bf16[1024,8192]{1,0:T(8,128)(2,1)} fusion(bf16[1024,512]{0,1:T(8,128)(2,1)S(1)} %bitcast.56, bf16[512,8192]{1,0:T(8,128)(2,1)} %param.13), kind=kOutput, calls=%fused_computation.12 | convolution fusion | flops 8598323200 | bytes 26214400 | tf_op jit(solution)/shard_map/dot_general | solution.py:113
  193.8 0.0 reduce-scatter.5.cloned.1.call-update
  193.8 0.0 copy-start.2
  193.9 24.1 %all-gather = bf16[8,1,512]{2,1,0:T(2,128)(2,1)S(1)} all-gather(bf16[1,1,512]{2,1,0:T(2,128)(2,1)S(1)} %reshape.99), channel_id=1, replica_groups=mesh['replica'=8,'tensor'=16] {'replica'}, dimensions={0}, use_global_device_ids=true | all-gather | bytes 9216 | tf_op jit(solution)/shard_map/all_gather | solution.py:87
  217.9 0.1 copy.40
  218.1 0.1 reshape.98
  218.2 0.0 all-gather.6.cloned.1.call-done
  218.2 2.8 copy.31
  221.0 1.8 reshape.97
  222.8 3.2 fusion.19
  226.0 1.7 reshape.95
  227.8 0.0 copy-done.2
  227.8 1.3 subtract_convert_fusion
  229.1 108.9 %reduce-scatter.5.cloned.1.call-done = bf16[64,8192]{1,0:T(8,128)(2,1)} async-done(((bf16[1024,8192]{1,0:T(8,128)(2,1)}), bf16[64,8192]{1,0:T(8,128)(2,1)}) %reduce-scatter.5.cloned.1.call-update) | async-done | bytes 1048592 | tf_op jit(solution)/shard_map/reduce_scatter | solution.py:112
  (3 shorter events, 0.0 us)
Async XLA Ops:
  8.0 58.6 %copy-start.4 = (f32[512,128]{1,0:T(8,128)S(1)}, f32[512,128]{1,0:T(8,128)}, u32[]{:S(2)}) copy-start(f32[512,128]{1,0:T(8,128)} %param.17) | copy-start | bytes 786436
  8.0 57.5 %reduce-scatter.7.cloned.1.call-start = ((), (), s32[]{:S(2)}) async-start(), calls=%async_computation.5 | async-start | bytes 1179648
  12.7 118.0 %all-gather.4.cloned.1.call-start = ((), (), s32[]{:S(2)}) async-start(), calls=%async_computation.2 | async-start | bytes 17825792 | tf_op jit(solution)/shard_map/all_gather | solution.py:101
  13.3 204.9 %all-gather.6.cloned.1.call-start = ((), (), s32[]{:S(2)}) async-start(), calls=%async_computation.4 | async-start | bytes 1179648 | tf_op jit(solution)/shard_map/all_gather | solution.py:86
  13.3 124.9 %collective-permute-start = (bf16[8192,128]{1,0:T(8,128)(2,1)}, bf16[8192,128]{1,0:T(8,128)(2,1)}, u32[]{:S(2)}, u32[]{:S(2)}) collective-permute-start(bf16[8192,128]{1,0:T(8,128)(2,1)} %param.12), channel_id=1, source_target_pairs={{0,1},{1,0},{2,3},{3,2},{4,5},{5,4},{6,7},{7,6},{8,9},{9,8},{10,11... | collective-permute-start | bytes 6291464 | tf_op jit(solution)/shard_map/ppermute | solution.py:19
  67.0 71.2 %copy-start.1 = (f32[512,128]{1,0:T(8,128)}, f32[512,128]{1,0:T(8,128)S(1)}, u32[]{:S(2)}) copy-start(f32[512,128]{1,0:T(8,128)S(1)} %get-tuple-element.7) | copy-start | bytes 786436
  68.2 70.0 %copy-start.5 = (f32[8192]{0:T(1024)S(1)}, f32[8192]{0:T(1024)}, u32[]{:S(2)}) copy-start(f32[8192]{0:T(1024)} %param.10) | copy-start | bytes 98308
  68.3 269.7 %reduce-scatter.5.cloned.1.call-start = ((), (), s32[]{:S(2)}) async-start(), calls=%async_computation.3 | async-start | bytes 17825792 | tf_op jit(solution)/shard_map/reduce_scatter | solution.py:112
  130.8 10.7 %copy-start = (bf16[1024,8192]{1,0:T(8,128)(2,1)S(1)}, bf16[1024,8192]{1,0:T(8,128)(2,1)}, u32[]{:S(2)}) copy-start(bf16[1024,8192]{1,0:T(8,128)(2,1)} %all-gather.4.cloned.1.call-done) | copy-start | bytes 50331652
  158.7 1.2 copy-start.3
  193.8 33.9 %copy-start.2 = (bf16[512,1024]{1,0:T(8,128)(2,1)S(1)}, bf16[512,1024]{1,0:T(8,128)(2,1)}, u32[]{:S(2)}) copy-start(bf16[512,1024]{1,0:T(8,128)(2,1)} %param.16) | copy-start | bytes 3145732
Sparse Core Ops, SparseCore 0:
  12.8 52.6 reduce-scatter.6
Sparse Core Ops, SparseCore 1:
  15.7 115.0 all-gather.3
  132.8 36.8 all-gather.5
  193.9 144.0 reduce-scatter.4
where the time goes:
time: 346 us
  waiting for transfers between devices  223 us (64%)
  matrix products  55.2 us (16%)
  blocking collectives  24.1 us (7%)
  between operations  15.9 us (5%)
  local copies, waits for them, and re-layouts  14.1 us (4%)
  other arithmetic  12.4 us (4%)
    reduce_scatter x1, waiting for transfers between devices, local(): lax.psum_scatter(jnp.dot(mixed, out_weight, preferred_element_type=jnp.fl...  109 us
    all_gather x1, waiting for transfers between devices, local(): lax.all_gather(tokens, 'tensor', axis=0, tiled=True)  62.3 us
    unnamed x5, waiting for transfers between devices  52.3 us
    all_gather x1, blocking collectives, local(): lax.all_gather(scales, 'replica', axis=1, tiled=True)  24.1 us
    dot_general x1, matrix products, local(): jnp.dot(normalize(lax.all_gather(tokens, 'tensor', axis=0, tiled=True), n...  17.3 us
    dot_general x1, matrix products, local(): jnp.dot(mixed, out_weight, preferred_element_type=jnp.float32)  16 us
    sub x1, matrix products, attend(): expo = jnp.exp(scores - peak)  10.6 us
    reduce_sum x1, other arithmetic, normalize(): power = jnp.mean(values * values, axis=-1, keepdims=True)  7.48 us
  transfers between devices with their start and end apart: 5, of which 3 were waited for; matrix products, arithmetic and copies ran while one was open for 21% of the time, Pallas kernels for 0%

commit v1 on v0

v1 whole, which is shorter than its diff:
```python
import functools
import math

import jax
import jax.numpy as jnp
from jax import lax
from jax.experimental import pallas as pl
from jax.experimental.pallas import tpu as pltpu
from jax.sharding import Mesh
from jax.sharding import PartitionSpec as P

HEAD = 128
REPLICA = ("x", "ylo")
TENSOR = ("yhi", "z", "core")
ROWS = 64
RING = (0, 1, -1, 2)
Y = ("ylo", "yhi")
HALVES = 2
MIB = 1024 * 1024


def params(mib=8):
    return pltpu.CompilerParams(vmem_limit_bytes=mib * MIB)


def cost(flops, moved):
    return pl.CostEstimate(flops=int(flops), bytes_accessed=int(moved), transcendentals=0)


def hadamard_table(width):
    index = jnp.arange(width, dtype=jnp.int32)
    common = jnp.bitwise_and(index[:, None], index[None, :])
    parity = jnp.zeros((width, width), jnp.int32)
    for bit in range(int(math.log2(width))):
        parity = parity + jnp.bitwise_and(jnp.right_shift(common, bit), 1)
    sign = 1.0 - 2.0 * jnp.bitwise_and(parity, 1).astype(jnp.float32)
    return sign / math.sqrt(width)


def norm_body(rows_ref, gain_ref, whole_ref, *half_refs):
    values = rows_ref[...].astype(jnp.float32)
    power = jnp.mean(values * values, axis=-1, keepdims=True)
    normed = (values * lax.rsqrt(power + 1e-05) * gain_ref[...]).astype(jnp.bfloat16)
    whole_ref[...] = normed
    count = normed.shape[0] // HALVES
    for at, half_ref in enumerate(half_refs):
        half_ref[...] = normed[at * count : (at + 1) * count]


def normalize(rows, gain):
    count, width = rows.shape
    return pl.pallas_call(
        norm_body,
        out_shape=[
            jax.ShapeDtypeStruct((c, width), jnp.bfloat16)
            for c in [count] + [count // HALVES] * HALVES
        ],
        compiler_params=params(12),
        cost_estimate=cost(4 * rows.size, 6 * rows.size),
        name="normalize",
    )(rows, gain.reshape(1, width))


def project_body(core_ref, *refs):
    blocks, refs = refs[:-7], refs[-7:]
    qa_ref, qb_ref, ka_ref, kb_ref, query_out, pair_out, total = refs
    step, steps = pl.program_id(0), pl.num_programs(0)
    half = qa_ref.shape[1]

    @pl.when(step == 0)
    def _():
        total[...] = jnp.zeros_like(total)

    rows = jnp.concatenate([ref[...] for ref in blocks], axis=0)
    both = jnp.concatenate([ka_ref[...], kb_ref[...]], axis=1)
    for start, weight in ((0, qa_ref[...]), (half, qb_ref[...]), (2 * half, both)):
        total[:, start : start + weight.shape[1]] += jnp.dot(
            rows, weight, preferred_element_type=jnp.float32
        )

    @pl.when(step == steps - 1)
    def _():
        flip = core_ref[0] == 0
        value = total[...].astype(jnp.bfloat16)
        query_out[...] = value[:, : 2 * half]
        left, right = value[:, 2 * half : 2 * half + HEAD], value[:, 2 * half + HEAD :]
        pair_out[:, :HEAD] = jnp.where(flip, left, right)
        pair_out[:, HEAD:] = jnp.where(flip, right, left)


def project(core, blocks, weights):
    width = blocks[0].shape[1]
    tile = 1024
    count = sum(block.shape[0] for block in blocks)
    qcols = 2 * weights[0].shape[1]
    kcols = 2 * weights[2].shape[1]
    smem = pl.BlockSpec(memory_space=pltpu.SMEM)
    whole = lambda cols: pl.BlockSpec((count, cols), lambda i: (0, 0))
    return pl.pallas_call(
        project_body,
        grid=(width // tile,),
        in_specs=[smem]
        + [pl.BlockSpec((block.shape[0], tile), lambda i: (0, i)) for block in blocks]
        + [pl.BlockSpec((tile, w.shape[1]), lambda i: (i, 0)) for w in weights],
        out_specs=[whole(qcols), whole(kcols)],
        out_shape=[
            jax.ShapeDtypeStruct((count, qcols), jnp.bfloat16),
            jax.ShapeDtypeStruct((count, kcols), jnp.bfloat16),
        ],
        scratch_shapes=[pltpu.VMEM((count, qcols + kcols), jnp.float32)],
        compiler_params=params(16),
        cost_estimate=cost(
            2 * 2 * count * width * (qcols + kcols), 2 * width * (count + qcols + kcols)
        ),
        name="project",
    )(core, *blocks, *weights)


def attend_body(core_ref, place_ref, *refs):
    *ins, mixed_ref, query_ref, own_ref, other_ref = refs
    core = core_ref[0]
    parts = len(ins) // 3
    for kind, whole in enumerate((query_ref, own_ref, other_ref)):
        slot = 0
        for part in ins[kind * parts : (kind + 1) * parts]:
            for top in range(0, part.shape[0], ROWS):
                place = pl.ds(pl.multiple_of(place_ref[slot] * ROWS, ROWS), ROWS)
                whole[place, :] = part[top : top + ROWS]
                slot += 1
    count, qcols = query_ref.shape
    heads = qcols // HEAD
    block = 2 * ROWS
    scale = 1.0 / math.sqrt(HEAD)
    shift = ROWS.bit_length() - 1
    for step in range(count // block):
        rows = slice(step * block, (step + 1) * block)
        span = (step + 1) * block
        query = jnp.concatenate(
            [query_ref[rows, h * HEAD : (h + 1) * HEAD] for h in range(heads)], axis=0
        )
        contract = (((1,), (1,)), ((), ()))
        row = lax.broadcasted_iota(jnp.int32, (block, block), 0)
        col = lax.broadcasted_iota(jnp.int32, (block, block), 1)
        own_seen = jnp.concatenate([col <= row] * heads, axis=0)
        other_seen = jnp.concatenate(
            [jnp.right_shift(col, shift) < jnp.right_shift(row, shift) + core] * heads, axis=0
        )

        def scores_of(ref, seen):
            raw = lax.dot_general(
                query, ref[:span, :HEAD], contract, preferred_element_type=jnp.float32
            )
            tail = jnp.where(seen, raw[:, span - block :], -jnp.inf)
            if span == block:
                return tail
            return jnp.concatenate([raw[:, : span - block], tail], axis=1)

        scores = jnp.concatenate(
            [scores_of(own_ref, own_seen), scores_of(other_ref, other_seen)], axis=1
        )
        peak = jnp.max(scores, axis=-1, keepdims=True)
        probs = jnp.exp((scores - peak) * scale).astype(jnp.bfloat16)
        ones = jnp.ones((span, HEAD), jnp.bfloat16)
        total = jnp.zeros((block * heads, 2 * HEAD), jnp.float32)
        for part, ref in enumerate((own_ref, other_ref)):
            values = jnp.concatenate([ref[:span, HEAD:], ones], axis=1)
            total += jnp.dot(
                probs[:, part * span : (part + 1) * span],
                values,
                preferred_element_type=jnp.float32,
            )
        mixed = (total[:, :HEAD] / total[:, HEAD:]).astype(jnp.bfloat16)
        for part in range(block // ROWS):
            slot = place_ref[8 + step * (block // ROWS) + part]
            place = pl.ds(pl.multiple_of(slot * ROWS, ROWS), ROWS)
            for h in range(heads):
                top = h * block + part * ROWS
                mixed_ref[place, h * HEAD : (h + 1) * HEAD] = mixed[top : top + ROWS]


def attend(core, places, queries, own, other):
    count, qcols = sum(q.shape[0] for q in queries), queries[0].shape[1]
    kcols = own[0].shape[1]
    args = [*queries, *own, *other]
    vmem = pl.BlockSpec(memory_space=pltpu.VMEM)
    return pl.pallas_call(
        attend_body,
        in_specs=[pl.BlockSpec(memory_space=pltpu.SMEM)] * 2 + [vmem] * len(args),
        out_specs=vmem,
        out_shape=jax.ShapeDtypeStruct((count, qcols), jnp.bfloat16),
        scratch_shapes=[pltpu.VMEM((count, cols), jnp.bfloat16) for cols in (qcols, kcols, kcols)],
        compiler_params=params(28),
        cost_estimate=cost(8 * count * count * qcols, 4 * count * qcols),
        name="attend",
    )(core, places, *args)


def output_body(first, mixed_ref, mine_ref, theirs_ref, *out_refs):
    half = mine_ref.shape[0]
    rows = mixed_ref[first : first + sum(ref.shape[0] for ref in out_refs)]
    result = (
        jnp.dot(rows[:, :half], mine_ref[...], preferred_element_type=jnp.float32)
        + jnp.dot(rows[:, half:], theirs_ref[...], preferred_element_type=jnp.float32)
    ).astype(jnp.bfloat16)
    top = 0
    for out_ref in out_refs:
        out_ref[...] = result[top : top + out_ref.shape[0]]
        top += out_ref.shape[0]


def output(mixed, mine, theirs, first, counts):
    width = mine.shape[1]
    depth = mixed.shape[1]
    count = sum(counts)
    tile = 1024
    weight = pl.BlockSpec((depth // 2, tile), lambda i: (0, i))
    return pl.pallas_call(
        functools.partial(output_body, first),
        grid=(width // tile,),
        in_specs=[pl.BlockSpec(mixed.shape, lambda i: (0, 0)), weight, weight],
        out_specs=[pl.BlockSpec((c, tile), lambda i: (0, i)) for c in counts],
        out_shape=[jax.ShapeDtypeStruct((c, width), jnp.bfloat16) for c in counts],
        compiler_params=params(16),
        cost_estimate=cost(2 * count * depth * width, 2 * (depth * width + count * width)),
        name="output",
    )(mixed, mine, theirs)


def pick_body(below_ref, above_ref, first_ref, second_ref):
    count = first_ref.shape[0]
    first_ref[...] = below_ref[:count]
    second_ref[...] = above_ref[count:]


def pick(below, above, flops):
    shape = jax.ShapeDtypeStruct((below.shape[0] // HALVES, below.shape[1]), below.dtype)
    return pl.pallas_call(
        pick_body,
        out_shape=[shape, shape],
        compiler_params=params(),
        cost_estimate=cost(flops, 4 * below.size),
        name="pick",
    )(below, above)


def split_body(*refs):
    terms, outs = refs[:-HALVES], refs[-HALVES:]
    count = outs[0].shape[0]
    for at, out_ref in enumerate(outs):
        rows = slice(at * count, (at + 1) * count)
        total = terms[0][rows].astype(jnp.float32)
        for ref in terms[1:]:
            total += ref[rows].astype(jnp.float32)
        out_ref[...] = total.astype(jnp.bfloat16)


def split_sum(*terms):
    shape = jax.ShapeDtypeStruct((terms[0].shape[0] // HALVES, terms[0].shape[1]), terms[0].dtype)
    return pl.pallas_call(
        split_body,
        out_shape=[shape] * HALVES,
        compiler_params=params(),
        cost_estimate=cost(3 * terms[0].size, 8 * terms[0].size),
        name="split",
    )(*terms)


def sums_body(shapes, *refs):
    outs, refs = refs[-len(shapes) :], refs[: -len(shapes)]
    first = 0
    for out_ref, starts in zip(outs, shapes):
        half = out_ref.shape[0] // HALVES
        for top in range(0, out_ref.shape[0], half):
            total = None
            for at, start in enumerate(starts):
                ref = refs[first + at]
                if start <= top < start + ref.shape[0]:
                    term = ref[top - start : top - start + half].astype(jnp.float32)
                    total = term if total is None else total + term
            out_ref[top : top + half] = total.astype(jnp.bfloat16)
        first += len(starts)


def sums(*groups, name="sums"):
    groups = [[t if isinstance(t, tuple) else (t, 0) for t in group] for group in groups]
    args = [array for group in groups for array, _ in group]
    shapes = tuple(tuple(start for _, start in group) for group in groups)
    result = pl.pallas_call(
        functools.partial(sums_body, shapes),
        out_shape=[jax.ShapeDtypeStruct(group[0][0].shape, jnp.bfloat16) for group in groups],
        compiler_params=params(16),
        cost_estimate=cost(sum(a.size for a in args), 3 * sum(a.size for a in args)),
        name=name,
    )(*args)
    return result if len(groups) > 1 else result[0]


def terms_body(block_ref, codes_ref, exps_ref, *out_refs):
    scale = jnp.exp2(exps_ref[...].astype(jnp.float32))
    lane = lax.broadcasted_iota(jnp.int32, scale.shape, 1)
    count = codes_ref.shape[0]
    for at, out_ref in enumerate(out_refs):
        for side in range(2):
            block = block_ref[2 * at + side]
            cols = pl.ds(pl.multiple_of(block * HEAD, HEAD), HEAD)
            mine = jnp.sum(jnp.where(lane == block, scale, 0.0), axis=1, keepdims=True)
            out_ref[side * count : (side + 1) * count] = (
                codes_ref[:, cols].astype(jnp.float32) * mine
            ).astype(jnp.bfloat16)


def terms(blocks, codes, exps):
    count, width = codes.shape
    vmem = pl.BlockSpec(memory_space=pltpu.VMEM)
    return pl.pallas_call(
        terms_body,
        in_specs=[pl.BlockSpec(memory_space=pltpu.SMEM), vmem, vmem],
        out_shape=[jax.ShapeDtypeStruct((2 * count, HEAD), jnp.bfloat16)] * len(RING),
        compiler_params=params(),
        cost_estimate=cost(codes.size, 4 * codes.size),
        name="terms",
    )(blocks, codes, exps)


def outer_body(replicas, *refs):
    mine_refs, theirs_ref, momentum_ref, table_ref, momentum_out, rebuilt_ref = (
        refs[:3],
        *refs[3:],
    )
    table = table_ref[...]

    def rotate(values):
        return jnp.dot(
            values, table, precision=lax.Precision.HIGHEST, preferred_element_type=jnp.float32
        )

    summed = theirs_ref[...].astype(jnp.float32)
    for ref in mine_refs:
        summed += ref[: summed.shape[0]].astype(jnp.float32)
    averaged = rotate(summed / replicas)
    fresh = 0.9 * momentum_ref[...] + averaged
    momentum_out[...] = fresh
    turned = rotate(0.7 * (averaged + 0.9 * fresh))
    scales = (jnp.max(jnp.abs(turned), axis=-1, keepdims=True) + 1e-06).astype(jnp.bfloat16)
    scales = scales.astype(jnp.float32)
    codes = (turned / scales).astype(jnp.bfloat16)
    rebuilt_ref[...] = rotate(codes.astype(jnp.float32) * scales).astype(jnp.bfloat16)


def outer(mine, theirs, momentum, table, replicas):
    return pl.pallas_call(
        functools.partial(outer_body, replicas),
        out_shape=[
            jax.ShapeDtypeStruct(momentum.shape, jnp.float32),
            jax.ShapeDtypeStruct(momentum.shape, jnp.bfloat16),
        ],
        compiler_params=params(),
        cost_estimate=cost(40 * theirs.size * HEAD, 12 * theirs.size),
        name="outer",
    )(*mine, theirs, momentum, table)


def apply_body(block_ref, params_ref, *refs):
    rebuilt_refs, out_ref = refs[:-1], refs[-1]
    count = out_ref.shape[0]
    for at, rebuilt_ref in enumerate(rebuilt_refs):
        for side in range(2):
            cols = pl.ds(pl.multiple_of(block_ref[2 * at + side] * HEAD, HEAD), HEAD)
            rebuilt = rebuilt_ref[side * count : (side + 1) * count].astype(jnp.float32)
            out_ref[:, cols] = (params_ref[:, cols].astype(jnp.float32) - rebuilt).astype(
                jnp.bfloat16
            )


def apply(blocks, old, rebuilt):
    vmem = pl.BlockSpec(memory_space=pltpu.VMEM)
    return pl.pallas_call(
        apply_body,
        in_specs=[pl.BlockSpec(memory_space=pltpu.SMEM)] + [vmem] * (1 + len(rebuilt)),
        out_shape=jax.ShapeDtypeStruct(old.shape, jnp.bfloat16),
        compiler_params=params(),
        cost_estimate=cost(old.size, 6 * old.size),
        name="apply",
    )(blocks, old, *rebuilt)


def swap(block, axis):
    return lax.ppermute(block, axis, [(0, 1), (1, 0)])


def hop(block, axis, way):
    at = (0, 2, 1, 3) if axis == Y else (0, 1, 2, 3)
    return lax.ppermute(block, axis, [(at[i], at[(i + way) % 4]) for i in range(4)])


def add(*blocks):
    total = blocks[0].astype(jnp.float32)
    for block in blocks[1:]:
        total = total + block.astype(jnp.float32)
    return total.astype(jnp.bfloat16)


def wait(*blocks):
    return lax.optimization_barrier(blocks)


def tie(block, *others):
    return lax.optimization_barrier((block, *others))[0]


def local(
    tokens, norm_gain, query_weight, kv_weight, out_weight, pseudo_grad, grad_exps, old, momentum
):
    core, z, yhi = lax.axis_index("core"), lax.axis_index("z"), lax.axis_index("yhi")
    x, ylo = lax.axis_index("x"), lax.axis_index("ylo")
    replicas = lax.axis_size(REPLICA)
    place = jnp.stack([(yhi ^ side) * 4 + (z + r) % 4 for side in range(2) for r in RING])
    chip = jnp.arange(8, dtype=jnp.int32)
    away = (chip % 4 - z) % 4
    slots = ((chip // 4) ^ yhi) * 4 + jnp.where(away < 2, away, 5 - away)
    share = jnp.stack([((x + r) % 4) * 2 + (ylo ^ side) for r in RING for side in range(2)])
    core, place, slots, share = (
        v.astype(jnp.int32).reshape(-1) for v in (core, place, slots, share)
    )
    places = jnp.concatenate([place, slots])

    block, h1, h2 = normalize(tokens, norm_gain)
    relay1, relay2 = hop(h1, Y, 1), hop(h2, Y, -1)
    below, above = hop(block, "z", 1), hop(block, "z", -1)
    kv_theirs = swap(tie(kv_weight, block), "core")
    at0, at1, at3, at2 = terms(share, tie(pseudo_grad[0], block), grad_exps[0])
    relay1, relay2, kv_theirs, at0, at1, at2, at3, query_weight = wait(
        relay1, relay2, kv_theirs, at0, at1, at2, at3, query_weight
    )
    query_theirs = swap(query_weight, "core")
    partner = jnp.concatenate([hop(relay1, Y, 1), hop(relay2, Y, -1)], axis=0)
    far1, far2 = pick(below, above, 1.5e11)
    partner = tie(partner, far1, far2)
    pbelow, pabove = hop(partner, "z", 1), hop(partner, "z", -1)
    far1, far2 = hop(far1, "z", 1), hop(far2, "z", -1)
    weights = [query_weight, query_theirs, kv_weight, kv_theirs]
    query_a, pair_a = project(core, [block, above, below, far1, far2], weights)
    x2 = hop(tie(at2, far1), "x", 1)
    pbelow, pabove, query_a, pair_a, x2, at1, at3, out_weight = wait(
        pbelow, pabove, query_a, pair_a, x2, at1, at3, out_weight
    )
    pfar1, pfar2 = pick(pbelow, pabove, 1e8)
    pfar1, pfar2 = hop(pfar1, "z", 1), hop(pfar2, "z", -1)
    passed, x3 = hop(add(at1, x2), "x", 1), hop(at3, "x", -1)
    query_m, pair_m = project(core, [partner, pabove, pbelow], weights)
    out_theirs = swap(out_weight, "core")
    pfar1, pfar2, query_m, pair_m, passed, x3, at0 = wait(
        pfar1, pfar2, query_m, pair_m, passed, x3, at0
    )
    other_a, other_m = swap(pair_a, "core"), swap(pair_m, "core")
    query_l, pair_l = project(core, [pfar1, pfar2], weights)
    other_l = swap(pair_l, "core")
    mine = (at0, passed, x3)
    count = momentum.shape[0]
    theirs = swap(add(*(part[count:] for part in mine)), "ylo")
    mixed = attend(
        core,
        places,
        (query_a, query_m, query_l),
        (pair_a, pair_m, pair_l),
        (other_a, other_m, other_l),
    )
    mixed, theirs, out_theirs = wait(mixed, theirs, out_theirs)

    half = ROWS // HALVES
    theirs_at = len(RING) * ROWS
    up1, down2 = output(mixed, out_weight, out_theirs, theirs_at + 3 * ROWS, [half] * HALVES)
    up1, down2 = hop(up1, "z", 1), hop(down2, "z", -1)
    new_momentum, rebuilt = outer(mine, theirs, momentum, hadamard_table(HEAD), replicas)
    beside = swap(rebuilt, "ylo")
    q0, qup, qdown = output(mixed, out_weight, out_theirs, theirs_at, [ROWS] * 3)
    up, down = sums((qup, (up1, 0)), (qdown, (down2, half)))
    both = jnp.concatenate([rebuilt, beside], axis=0)
    up, down, both, mixed = wait(up, down, both, mixed)
    up, down = hop(up, "z", 1), hop(down, "z", -1)
    before = hop(both, "x", 1)
    o0, oup, odown, ofar1, ofar2 = output(
        mixed, out_weight, out_theirs, 0, [ROWS] * 3 + [half] * HALVES
    )
    far1, far2 = hop(ofar1, "z", 1), hop(ofar2, "z", -1)
    after = hop(tie(both, before), "x", -1)
    up, down, before, after, oup, odown = wait(up, down, before, after, oup, odown)
    s1, s2 = split_sum(q0, up, down)
    s1, s2 = hop(s1, Y, 1), hop(s2, Y, -1)
    ahead = hop(before, "x", 1)
    oup, odown = sums((oup, (far1, 0)), (odown, (far2, half)))
    up, down = hop(oup, "z", 1), hop(odown, "z", -1)
    s1, s2, ahead = wait(s1, s2, ahead)
    s1, s2 = hop(s1, Y, 1), hop(s2, Y, -1)
    new_params = apply(share, old, [both, after, before, ahead])
    o0, new_params = wait(o0, new_params)
    attended = sums((o0, up, down, (s1, 0), (s2, half)), name="finish")
    return (attended, new_params, new_momentum)


def solution(mesh):
    fine = Mesh(mesh.devices.reshape(4, 2, 2, 4, 2), ("x", "ylo", "yhi", "z", "core"))
    every = REPLICA + TENSOR
    return jax.shard_map(
        local,
        mesh=fine,
        in_specs=(
            P(every, None),
            P(),
            P(None, TENSOR),
            P(None, TENSOR),
            P(TENSOR, None),
            P(REPLICA, TENSOR, None),
            P(REPLICA, TENSOR, None),
            P(TENSOR, None),
            P(TENSOR, REPLICA),
        ),
        out_specs=(P(every, None), P(TENSOR, None), P(TENSOR, REPLICA)),
        check_vma=False,
    )
```

time: 346 us -> 202 us (0.58)
  waiting for transfers between devices: 223 us -> 52.8 us
  Pallas kernels: 0 us -> 76.3 us
  matrix products: 55.2 us -> 0 us
  starting transfers between devices: 0.43 us -> 51.7 us
  blocking collectives: 24.1 us -> 0 us
  between operations: 15.9 us -> 1.06 us
  other arithmetic: 12.4 us -> 2.46 us
    reduce_scatter x1 -> x0, waiting for transfers between devices: 109 us -> none  [local(): lax.psum_scatter(jnp.dot(mixed, out_weight, preferred_element_type=jnp.fl...]
    pallas_call x0 -> x17, Pallas kernels: none -> 76.3 us  [the longest x3 29.6 us: output(): pl.pallas_call(functools.partial(output_body, first), grid=(width // tile...]
    all_gather x2 -> x0, waiting for transfers between devices: 62.3 us -> none  [the longest x1 62.3 us: local(): lax.all_gather(tokens, 'tensor', axis=0, tiled=True)]
    ppermute x1 -> x38, waiting for transfers between devices: 0.01 us -> 52.8 us  [the longest x30 52.8 us: hop(): lax.ppermute(block, axis, [(at[i], at[(i + way) % 4]) for i in range(4)])]
    unnamed x5 -> x0, waiting for transfers between devices: 52.3 us -> none
    ppermute x1 -> x38, starting transfers between devices: 0.09 us -> 51.7 us  [the longest x30 48.2 us: hop(): lax.ppermute(block, axis, [(at[i], at[(i + way) % 4]) for i in range(4)])]
    dot_general x6 -> x0, matrix products: 44.6 us -> none  [the longest x1 17.3 us: local(): jnp.dot(normalize(lax.all_gather(tokens, 'tensor', axis=0, tiled=True), n...]
    all_gather x1 -> x0, blocking collectives: 24.1 us -> none  [local(): lax.all_gather(scales, 'replica', axis=1, tiled=True)]
  transfers between devices with their start and end apart: 5 -> 38, of which waited for: 3 -> 11; matrix products, arithmetic and copies ran while one was open for 21% -> 2% of each run, Pallas kernels for 0% -> 32%
where the time goes in v1:
time: 202 us; the launch traced here: 201 us
  Pallas kernels  76.3 us (38%)
  waiting for transfers between devices  52.8 us (26%)
  starting transfers between devices  51.7 us (26%)
  local copies, waits for them, and re-layouts  16.4 us (8%)
  other arithmetic  2.46 us (1%)
    ppermute x30, waiting for transfers between devices, hop(): lax.ppermute(block, axis, [(at[i], at[(i + way) % 4]) for i in range(4)])  52.8 us
    ppermute x30, starting transfers between devices, hop(): lax.ppermute(block, axis, [(at[i], at[(i + way) % 4]) for i in range(4)])  48.2 us
    pallas_call x3, Pallas kernels, output(): pl.pallas_call(functools.partial(output_body, first), grid=(width // tile...  29.6 us
    pallas_call x3, Pallas kernels, project(): pl.pallas_call(project_body, grid=(width // tile,), in_specs=[smem] + [pl...  28.3 us
    unnamed x43, local copies, waits for them, and re-layouts  16.3 us
    pallas_call x1, Pallas kernels, attend(): pl.pallas_call(attend_body, in_specs=[pl.BlockSpec(memory_space=pltpu.SME...  5.42 us
    pallas_call x2, Pallas kernels, pick(): pl.pallas_call(pick_body, out_shape=[shape, shape], compiler_params=param...  4.31 us
  transfers between devices with their start and end apart: 38, of which 11 were waited for; matrix products, arithmetic and copies ran while one was open for 2% of the time, Pallas kernels for 32%

profile of v1, /device:TPU:0, one launch (start us, length us, event | category | flops | bytes accessed | tf_op | source)
XLA Modules:
  0.0 200.7 jit_solution(17779399151618272563)
XLA Ops:
  0.7 1.3 copy-done.7
  2.0 0.8 copy-done.14
  2.7 1.8 normalize.1
  4.5 2.0 collective-permute-start.5
  6.5 2.1 %collective-permute-start.6 = (bf16[64,8192]{1,0:T(8,128)(2,1)}, bf16[64,8192]{1,0:T(8,128)(2,1)}, u32[]{:S(2)}, u32[]{:S(2)}) collective-permute-start(bf16[64,8192]{1,0:T(8,128)(2,1)} %get-tuple-element.86.refs_0_), channel_id=1, source_target_pairs={{0,6},{2,0},{4,2},{6,4},{1,7},{3,1},{5,3},{7,5},{8,14},{10,8},{12,... | collective-permute-start | bytes 3145736 | tf_op jit(solution)/shard_map/ppermute | solution.py:393
  8.7 1.6 collective-permute-start
  10.2 1.7 collective-permute-start.1
  11.9 0.8 copy.12
  12.8 1.2 terms.1
  14.0 0.7 copy-done.9
  14.7 0.7 copy-done.12
  15.4 0.7 copy-done.15
  16.2 0.7 copy-done.17
  16.9 7.4 %collective-permute-done = bf16[32,8192]{1,0:T(8,128)(2,1)} collective-permute-done((bf16[32,8192]{1,0:T(8,128)(2,1)}, bf16[32,8192]{1,0:T(8,128)(2,1)}, u32[]{:S(2)}, u32[]{:S(2)}) %collective-permute-start) | collective-permute-done | bytes 524320 | tf_op jit(solution)/shard_map/ppermute | solution.py:393
  24.3 1.3 copy-done.3
  25.7 2.9 %collective-permute-start.4 = (bf16[32,8192]{1,0:T(8,128)(2,1)}, bf16[32,8192]{1,0:T(8,128)(2,1)}, u32[]{:S(2)}, u32[]{:S(2)}) collective-permute-start(bf16[32,8192]{1,0:T(8,128)(2,1)} %collective-permute-done.1), channel_id=1, source_target_pairs={{0,24},{16,0},{8,16},{24,8},{1,25},{17,1},{9,17},{25,9},{2,26},{18... | collective-permute-start | bytes 1572872 | tf_op jit(solution)/shard_map/ppermute | solution.py:393
  28.6 4.2 %collective-permute-done.5.below_ref.refs_2_ = bf16[64,8192]{1,0:T(8,128)(2,1)} collective-permute-done((bf16[64,8192]{1,0:T(8,128)(2,1)}, bf16[64,8192]{1,0:T(8,128)(2,1)}, u32[]{:S(2)}, u32[]{:S(2)}) %collective-permute-start.5) | collective-permute-done | bytes 1048608 | tf_op jit(solution)/shard_map/ppermute | solution.py:393
  32.8 2.5 %pick.2 = (bf16[32,8192]{1,0:T(8,128)(2,1)}, bf16[32,8192]{1,0:T(8,128)(2,1)}) custom-call(bf16[64,8192]{1,0:T(8,128)(2,1)} %collective-permute-done.5.below_ref.refs_2_, bf16[64,8192]{1,0:T(8,128)(2,1)} %collective-permute-done.6.above_ref.refs_1_), custom_call_target="tpu_custom_call" | custom-call | flops 149999992832 | bytes 2097152 | tf_op jit(solution)/shard_map/pick/pallas_call | solution.py:237
  35.4 1.3 collective-permute-start.9
  36.6 2.0 collective-permute-start.10
  38.6 0.8 collective-permute-done.4
  39.4 3.4 %collective-permute-done.3 = bf16[32,8192]{1,0:T(8,128)(2,1)} collective-permute-done((bf16[32,8192]{1,0:T(8,128)(2,1)}, bf16[32,8192]{1,0:T(8,128)(2,1)}, u32[]{:S(2)}, u32[]{:S(2)}) %collective-permute-start.3) | collective-permute-done | bytes 524320 | tf_op jit(solution)/shard_map/ppermute | solution.py:393
  42.8 1.3 pad_maximum_fusion.refs_0_
  44.2 3.2 %collective-permute-start.8 = (bf16[64,8192]{1,0:T(8,128)(2,1)S(1)}, bf16[64,8192]{1,0:T(8,128)(2,1)}, u32[]{:S(2)}, u32[]{:S(2)}) collective-permute-start(bf16[64,8192]{1,0:T(8,128)(2,1)S(1)} %pad_maximum_fusion.refs_0_), channel_id=1, source_target_pairs={{0,6},{2,0},{4,2},{6,4},{1,7},{3,1},{5,3},{7,5},{8,14},{10,8},{12,... | collective-permute-start | bytes 3145736 | tf_op jit(solution)/shard_map/ppermute | solution.py:393
  47.4 4.3 %collective-permute-done.9.refs_3_ = bf16[32,8192]{1,0:T(8,128)(2,1)} collective-permute-done((bf16[32,8192]{1,0:T(8,128)(2,1)}, bf16[32,8192]{1,0:T(8,128)(2,1)}, u32[]{:S(2)}, u32[]{:S(2)}) %collective-permute-start.9) | collective-permute-done | bytes 524320 | tf_op jit(solution)/shard_map/ppermute | solution.py:393
  51.7 1.5 collective-permute-start.12
  53.2 3.4 %copy-done = bf16[8192,512]{1,0:T(8,128)(2,1)S(1)} copy-done((bf16[8192,512]{1,0:T(8,128)(2,1)S(1)}, bf16[8192,512]{1,0:T(8,128)(2,1)}, u32[]{:S(2)}) %copy-start) | copy-done | bytes 8388632
  56.6 1.6 copy-done.4
  58.2 10.6 %project.3 = (bf16[256,1024]{1,0:T(8,128)(2,1)S(1)}, bf16[256,256]{1,0:T(8,128)(2,1)S(1)}) custom-call(s32[1]{0:T(128)} %bitcast.core_ref, bf16[64,8192]{1,0:T(8,128)(2,1)} %get-tuple-element.86.refs_0_, bf16[64,8192]{1,0:T(8,128)(2,1)} %collective-permute-done.6.above_ref.refs_1_, bf16[64,8192]{1,0:T(8,128)(2,1)} %collective-permute-done.5.below_ref.refs_2_, ...), custom_call_target="tpu_custom_call" | custom-call | flops 10737418240 | bytes 25165824 | tf_op jit(solution)/shard_map/project/pallas_call | solution.py:99
  68.8 0.8 copy-done.18
  69.6 3.5 %collective-permute-done.7.below_ref.refs_2_ = bf16[64,8192]{1,0:T(8,128)(2,1)} collective-permute-done((bf16[64,8192]{1,0:T(8,128)(2,1)S(1)}, bf16[64,8192]{1,0:T(8,128)(2,1)}, u32[]{:S(2)}, u32[]{:S(2)}) %collective-permute-start.7) | collective-permute-done | bytes 1048608 | tf_op jit(solution)/shard_map/ppermute | solution.py:393
  73.3 1.8 pick.3
  75.1 0.9 collective-permute-start.13
  76.0 2.4 %collective-permute-start.14 = (bf16[32,8192]{1,0:T(8,128)(2,1)S(1)}, bf16[32,8192]{1,0:T(8,128)(2,1)S(1)}, u32[]{:S(2)}, u32[]{:S(2)}) collective-permute-start(bf16[32,8192]{1,0:T(8,128)(2,1)S(1)} %get-tuple-element.110), channel_id=1, source_target_pairs={{0,6},{2,0},{4,2},{6,4},{1,7},{3,1},{5,3},{7,5},{8,14},{10,8},{12,... | collective-permute-start | bytes 1572872 | tf_op jit(solution)/shard_map/ppermute | solution.py:393
  78.4 1.0 add_convert_fusion
  79.4 1.6 collective-permute-start.15
  81.0 1.7 collective-permute-start.16
  82.7 3.4 %copy-done.1 = bf16[8192,512]{1,0:T(8,128)(2,1)S(1)} copy-done((bf16[8192,512]{1,0:T(8,128)(2,1)S(1)}, bf16[8192,512]{1,0:T(8,128)(2,1)}, u32[]{:S(2)}) %copy-start.1) | copy-done | bytes 8388632
  86.1 9.5 %project.4 = (bf16[192,1024]{1,0:T(8,128)(2,1)S(1)}, bf16[192,256]{1,0:T(8,128)(2,1)S(1)}) custom-call(s32[1]{0:T(128)} %bitcast.core_ref, bf16[64,8192]{1,0:T(8,128)(2,1)S(1)} %pad_maximum_fusion.refs_0_, bf16[64,8192]{1,0:T(8,128)(2,1)} %collective-permute-done.8.above_ref.refs_1_, bf16[64,8192]{1,0:T(8,128)(2,1)} %collective-permute-done.7.below_ref.refs_2_, ...), custom_call_target="tpu_custom_call" | custom-call | flops 8053063680 | bytes 24117248 | tf_op jit(solution)/shard_map/project/pallas_call | solution.py:99
  95.7 0.6 collective-permute-start.18
  96.3 8.2 %project.5 = (bf16[64,1024]{1,0:T(8,128)(2,1)S(1)}, bf16[64,256]{1,0:T(8,128)(2,1)S(1)}) custom-call(s32[1]{0:T(128)} %bitcast.core_ref, bf16[32,8192]{1,0:T(8,128)(2,1)S(1)} %collective-permute-done.13.refs_0_, bf16[32,8192]{1,0:T(8,128)(2,1)S(1)} %collective-permute-done.14.refs_1_, bf16[8192,512]{1,0:T(8,128)(2,1)S(1)} %copy-done.1, ...), custom_call_target="tpu_custom_call" | custom-call | flops 2684354560 | bytes 22020096 | tf_op jit(solution)/shard_map/project/pallas_call | solution.py:99
  104.8 1.8 collective-permute-start.20
  106.6 5.4 %attend.1.mixed_ref = bf16[512,1024]{1,0:T(8,128)(2,1)S(1)} custom-call(s32[1]{0:T(128)} %bitcast.core_ref, s32[16]{0:T(128)S(1)} %concatenate.9.place_ref, bf16[256,1024]{1,0:T(8,128)(2,1)S(1)} %copy-done.19, bf16[192,1024]{1,0:T(8,128)(2,1)S(1)} %get-tuple-element.117.refs_1_, bf16[64,1024]{1,0:T(8,128)(2,1)S(1)} %get-tuple-element.120.refs_2_, ...), custom_call_target="tpu_custom_call" | custom-call | flops 2147483648 | bytes 2097152 | tf_op jit(solution)/shard_map/attend/pallas_call | solution.py:186
  112.1 9.3 %output.4 = (bf16[32,8192]{1,0:T(8,128)(2,1)S(1)}, bf16[32,8192]{1,0:T(8,128)(2,1)S(1)}) custom-call(bf16[512,1024]{1,0:T(8,128)(2,1)S(1)} %attend.1.mixed_ref, bf16[512,8192]{1,0:T(8,128)(2,1)} %mine_ref.2, bf16[512,8192]{1,0:T(8,128)(2,1)} %collective-permute-done.21.theirs_ref), custom_call_target="tpu_custom_call" | custom-call | flops 1073741824 | bytes 17825792 | tf_op jit(solution)/shard_map/output/pallas_call | solution.py:217
  121.5 3.2 %collective-permute-start.23 = (bf16[32,8192]{1,0:T(8,128)(2,1)S(1)}, bf16[32,8192]{1,0:T(8,128)(2,1)S(1)}, u32[]{:S(2)}, u32[]{:S(2)}) collective-permute-start(bf16[32,8192]{1,0:T(8,128)(2,1)S(1)} %get-tuple-element.133), channel_id=1, source_target_pairs={{0,6},{2,0},{4,2},{6,4},{1,7},{3,1},{5,3},{7,5},{8,14},{10,8},{12,... | collective-permute-start | bytes 1572872 | tf_op jit(solution)/shard_map/ppermute | solution.py:393
  124.8 1.5 outer.1
  126.3 0.8 collective-permute-start.24
  127.1 9.8 %output.3 = (bf16[64,8192]{1,0:T(8,128)(2,1)S(1)}, bf16[64,8192]{1,0:T(8,128)(2,1)S(1)}, bf16[64,8192]{1,0:T(8,128)(2,1)S(1)}) custom-call(bf16[512,1024]{1,0:T(8,128)(2,1)S(1)} %attend.1.mixed_ref, bf16[512,8192]{1,0:T(8,128)(2,1)} %mine_ref.2, bf16[512,8192]{1,0:T(8,128)(2,1)} %collective-permute-done.21.theirs_ref), custom_call_target="tpu_custom_call" | custom-call | flops 3221225472 | bytes 19922944 | tf_op jit(solution)/shard_map/output/pallas_call | solution.py:217
  137.4 3.2 %collective-permute-start.26 = (bf16[64,8192]{1,0:T(8,128)(2,1)S(1)}, bf16[64,8192]{1,0:T(8,128)(2,1)S(1)}, u32[]{:S(2)}, u32[]{:S(2)}) collective-permute-start(bf16[64,8192]{1,0:T(8,128)(2,1)S(1)} %get-tuple-element.142), channel_id=1, source_target_pairs={{0,6},{2,0},{4,2},{6,4},{1,7},{3,1},{5,3},{7,5},{8,14},{10,8},{12,... | collective-permute-start | bytes 3145736 | tf_op jit(solution)/shard_map/ppermute | solution.py:393
  140.9 10.4 %output.5 = (bf16[64,8192]{1,0:T(8,128)(2,1)S(1)}, bf16[64,8192]{1,0:T(8,128)(2,1)S(1)}, bf16[64,8192]{1,0:T(8,128)(2,1)S(1)}, bf16[32,8192]{1,0:T(8,128)(2,1)S(1)}, bf16[32,8192]{1,0:T(8,128)(2,1)S(1)}) custom-call(bf16[512,1024]{1,0:T(8,128)(2,1)S(1)} %attend.1.mixed_ref, bf16[512,8192]{1,0:T(8,128)(2,1)} %mine_ref.2, ...), custom_call_target="tpu_custom_call" | custom-call | flops 4294967296 | bytes 20971520 | tf_op jit(solution)/shard_map/output/pallas_call | solution.py:217
  151.4 3.2 %collective-permute-start.33 = (bf16[32,8192]{1,0:T(8,128)(2,1)S(1)}, bf16[32,8192]{1,0:T(8,128)(2,1)S(1)}, u32[]{:S(2)}, u32[]{:S(2)}) collective-permute-start(bf16[32,8192]{1,0:T(8,128)(2,1)S(1)} %get-tuple-element.158), channel_id=1, source_target_pairs={{0,6},{2,0},{4,2},{6,4},{1,7},{3,1},{5,3},{7,5},{8,14},{10,8},{12,... | collective-permute-start | bytes 1572872 | tf_op jit(solution)/shard_map/ppermute | solution.py:393
  154.6 3.0 %collective-permute-start.28 = (bf16[1024,128]{1,0:T(8,128)(2,1)S(1)}, bf16[1024,128]{1,0:T(8,128)(2,1)S(1)}, u32[]{:S(2)}, u32[]{:S(2)}) collective-permute-start(bf16[1024,128]{1,0:T(8,128)(2,1)S(1)} %pad_maximum_fusion.1.refs_0_), channel_id=1, source_target_pairs={{0,96},{32,0},{64,32},{96,64},{1,97},{33,1},{65,33},{97,65},{2,98}... | collective-permute-start | bytes 786440 | tf_op jit(solution)/shard_map/ppermute | solution.py:393
  157.6 3.9 %collective-permute-done.28.refs_1_ = bf16[1024,128]{1,0:T(8,128)(2,1)S(1)} collective-permute-done((bf16[1024,128]{1,0:T(8,128)(2,1)S(1)}, bf16[1024,128]{1,0:T(8,128)(2,1)S(1)}, u32[]{:S(2)}, u32[]{:S(2)}) %collective-permute-start.28) | collective-permute-done | bytes 262176 | tf_op jit(solution)/shard_map/ppermute | solution.py:393
  161.4 3.2 %collective-permute-done.25.refs_1_ = bf16[64,8192]{1,0:T(8,128)(2,1)S(1)} collective-permute-done((bf16[64,8192]{1,0:T(8,128)(2,1)S(1)}, bf16[64,8192]{1,0:T(8,128)(2,1)S(1)}, u32[]{:S(2)}, u32[]{:S(2)}) %collective-permute-start.25) | collective-permute-done | bytes 1048608 | tf_op jit(solution)/shard_map/ppermute | solution.py:393
  165.0 1.3 collective-permute-start.29
  166.4 2.0 collective-permute-start.30
  168.4 5.8 %collective-permute-done.32.refs_1_ = bf16[32,8192]{1,0:T(8,128)(2,1)S(1)} collective-permute-done((bf16[32,8192]{1,0:T(8,128)(2,1)S(1)}, bf16[32,8192]{1,0:T(8,128)(2,1)S(1)}, u32[]{:S(2)}, u32[]{:S(2)}) %collective-permute-start.32) | collective-permute-done | bytes 524320 | tf_op jit(solution)/shard_map/ppermute | solution.py:393
  175.0 2.8 %collective-permute-start.35 = (bf16[64,8192]{1,0:T(8,128)(2,1)S(1)}, bf16[64,8192]{1,0:T(8,128)(2,1)S(1)}, u32[]{:S(2)}, u32[]{:S(2)}) collective-permute-start(bf16[64,8192]{1,0:T(8,128)(2,1)S(1)} %get-tuple-element.160), channel_id=1, source_target_pairs={{0,6},{2,0},{4,2},{6,4},{1,7},{3,1},{5,3},{7,5},{8,14},{10,8},{12,... | collective-permute-start | bytes 3145736 | tf_op jit(solution)/shard_map/ppermute | solution.py:393
  178.1 7.3 %collective-permute-done.31.refs_3_ = bf16[1024,128]{1,0:T(8,128)(2,1)S(1)} collective-permute-done((bf16[1024,128]{1,0:T(8,128)(2,1)S(1)}, bf16[1024,128]{1,0:T(8,128)(2,1)S(1)}, u32[]{:S(2)}, u32[]{:S(2)}) %collective-permute-start.31) | collective-permute-done | bytes 262176 | tf_op jit(solution)/shard_map/ppermute | solution.py:393
  185.4 1.2 collective-permute-start.36
  186.6 2.0 collective-permute-start.37
  188.6 1.8 apply.1
  190.5 8.8 %collective-permute-done.34.refs_1_ = bf16[64,8192]{1,0:T(8,128)(2,1)S(1)} collective-permute-done((bf16[64,8192]{1,0:T(8,128)(2,1)S(1)}, bf16[64,8192]{1,0:T(8,128)(2,1)S(1)}, u32[]{:S(2)}, u32[]{:S(2)}) %collective-permute-start.34) | collective-permute-done | bytes 1048608 | tf_op jit(solution)/shard_map/ppermute | solution.py:393
  199.3 1.5 finish.1
  (80 shorter events, 3.1 us)
Async XLA Ops:
  0.6 12.2 %copy-start.6 = (bf16[1,512,1024]{2,1,0:T(8,128)(2,1)S(1)}, bf16[1,512,1024]{2,1,0:T(8,128)(2,1)}, u32[]{:S(2)}) copy-start(bf16[1,512,1024]{2,1,0:T(8,128)(2,1)} %param.14) | copy-start | bytes 3145732
  0.6 1.3 copy-start.7
  2.0 0.8 copy-start.14
  4.5 19.8 %collective-permute-start.2 = (bf16[8192,128]{1,0:T(8,128)(2,1)}, bf16[8192,128]{1,0:T(8,128)(2,1)S(1)}, u32[]{:S(2)}, u32[]{:S(2)}) collective-permute-start(bf16[8192,128]{1,0:T(8,128)(2,1)} %refs_4_.2), channel_id=1, source_target_pairs={{0,1},{1,0},{2,3},{3,2},{4,5},{5,4},{6,7},{7,6},{8,9},{9,8},{10,11... | collective-permute-start | bytes 6291464 | tf_op jit(solution)/shard_map/ppermute | solution.py:388
  4.5 28.3 %collective-permute-start.5 = (bf16[64,8192]{1,0:T(8,128)(2,1)}, bf16[64,8192]{1,0:T(8,128)(2,1)}, u32[]{:S(2)}, u32[]{:S(2)}) collective-permute-start(bf16[64,8192]{1,0:T(8,128)(2,1)} %get-tuple-element.86.refs_0_), channel_id=1, source_target_pairs={{0,2},{2,4},{4,6},{6,0},{1,3},{3,5},{5,7},{7,1},{8,10},{10,12},{12... | collective-permute-start | bytes 3145736 | tf_op jit(solution)/shard_map/ppermute | solution.py:393
  6.5 26.3 %collective-permute-start.6 = (bf16[64,8192]{1,0:T(8,128)(2,1)}, bf16[64,8192]{1,0:T(8,128)(2,1)}, u32[]{:S(2)}, u32[]{:S(2)}) collective-permute-start(bf16[64,8192]{1,0:T(8,128)(2,1)} %get-tuple-element.86.refs_0_), channel_id=1, source_target_pairs={{0,6},{2,0},{4,2},{6,4},{1,7},{3,1},{5,3},{7,5},{8,14},{10,8},{12,... | collective-permute-start | bytes 3145736 | tf_op jit(solution)/shard_map/ppermute | solution.py:393
  8.7 15.6 %collective-permute-start = (bf16[32,8192]{1,0:T(8,128)(2,1)}, bf16[32,8192]{1,0:T(8,128)(2,1)}, u32[]{:S(2)}, u32[]{:S(2)}) collective-permute-start(bf16[32,8192]{1,0:T(8,128)(2,1)} %get-tuple-element.84), channel_id=1, source_target_pairs={{0,16},{16,8},{8,24},{24,0},{1,17},{17,9},{9,25},{25,1},{2,18},{18... | collective-permute-start | bytes 1572872 | tf_op jit(solution)/shard_map/ppermute | solution.py:393
  10.2 14.1 %collective-permute-start.1 = (bf16[32,8192]{1,0:T(8,128)(2,1)}, bf16[32,8192]{1,0:T(8,128)(2,1)}, u32[]{:S(2)}, u32[]{:S(2)}) collective-permute-start(bf16[32,8192]{1,0:T(8,128)(2,1)} %get-tuple-element.85), channel_id=1, source_target_pairs={{0,24},{16,0},{8,16},{24,8},{1,25},{17,1},{9,17},{25,9},{2,26},{18... | collective-permute-start | bytes 1572872 | tf_op jit(solution)/shard_map/ppermute | solution.py:393
  14.0 0.7 copy-start.9
  14.7 0.7 copy-start.12
  15.4 0.7 copy-start.15
  16.2 0.7 copy-start.17
  24.3 1.3 copy-start.3
  25.7 13.8 %collective-permute-start.4 = (bf16[32,8192]{1,0:T(8,128)(2,1)}, bf16[32,8192]{1,0:T(8,128)(2,1)}, u32[]{:S(2)}, u32[]{:S(2)}) collective-permute-start(bf16[32,8192]{1,0:T(8,128)(2,1)} %collective-permute-done.1), channel_id=1, source_target_pairs={{0,24},{16,0},{8,16},{24,8},{1,25},{17,1},{9,17},{25,9},{2,26},{18... | collective-permute-start | bytes 1572872 | tf_op jit(solution)/shard_map/ppermute | solution.py:393
  28.6 14.2 %collective-permute-start.3 = (bf16[32,8192]{1,0:T(8,128)(2,1)}, bf16[32,8192]{1,0:T(8,128)(2,1)}, u32[]{:S(2)}, u32[]{:S(2)}) collective-permute-start(bf16[32,8192]{1,0:T(8,128)(2,1)} %collective-permute-done), channel_id=1, source_target_pairs={{0,16},{16,8},{8,24},{24,0},{1,17},{17,9},{9,25},{25,1},{2,18},{18... | collective-permute-start | bytes 1572872 | tf_op jit(solution)/shard_map/ppermute | solution.py:393
  28.6 24.6 %collective-permute-start.11 = (bf16[8192,512]{1,0:T(8,128)(2,1)}, bf16[8192,512]{1,0:T(8,128)(2,1)}, u32[]{:S(2)}, u32[]{:S(2)}) collective-permute-start(bf16[8192,512]{1,0:T(8,128)(2,1)} %refs_2_), channel_id=1, source_target_pairs={{0,1},{1,0},{2,3},{3,2},{4,5},{5,4},{6,7},{7,6},{8,9},{9,8},{10,11... | collective-permute-start | bytes 25165832 | tf_op jit(solution)/shard_map/ppermute | solution.py:388
  35.4 17.8 %copy-start.2 = (bf16[8192,128]{1,0:T(8,128)(2,1)S(1)}, bf16[8192,128]{1,0:T(8,128)(2,1)}, u32[]{:S(2)}) copy-start(bf16[8192,128]{1,0:T(8,128)(2,1)} %refs_4_.2) | copy-start | bytes 6291460
  35.4 16.3 %collective-permute-start.9 = (bf16[32,8192]{1,0:T(8,128)(2,1)}, bf16[32,8192]{1,0:T(8,128)(2,1)}, u32[]{:S(2)}, u32[]{:S(2)}) collective-permute-start(bf16[32,8192]{1,0:T(8,128)(2,1)} %get-tuple-element.95), channel_id=1, source_target_pairs={{0,2},{2,4},{4,6},{6,0},{1,3},{3,5},{5,7},{7,1},{8,10},{10,12},{12... | collective-permute-start | bytes 1572872 | tf_op jit(solution)/shard_map/ppermute | solution.py:393
  36.6 16.6 %collective-permute-start.10 = (bf16[32,8192]{1,0:T(8,128)(2,1)}, bf16[32,8192]{1,0:T(8,128)(2,1)}, u32[]{:S(2)}, u32[]{:S(2)}) collective-permute-start(bf16[32,8192]{1,0:T(8,128)(2,1)} %get-tuple-element.96), channel_id=1, source_target_pairs={{0,6},{2,0},{4,2},{6,4},{1,7},{3,1},{5,3},{7,5},{8,14},{10,8},{12,... | collective-permute-start | bytes 1572872 | tf_op jit(solution)/shard_map/ppermute | solution.py:393
  44.1 29.0 %collective-permute-start.7 = (bf16[64,8192]{1,0:T(8,128)(2,1)S(1)}, bf16[64,8192]{1,0:T(8,128)(2,1)}, u32[]{:S(2)}, u32[]{:S(2)}) collective-permute-start(bf16[64,8192]{1,0:T(8,128)(2,1)S(1)} %pad_maximum_fusion.refs_0_), channel_id=1, source_target_pairs={{0,2},{2,4},{4,6},{6,0},{1,3},{3,5},{5,7},{7,1},{8,10},{10,12},{12... | collective-permute-start | bytes 3145736 | tf_op jit(solution)/shard_map/ppermute | solution.py:393
  44.2 28.9 %collective-permute-start.8 = (bf16[64,8192]{1,0:T(8,128)(2,1)S(1)}, bf16[64,8192]{1,0:T(8,128)(2,1)}, u32[]{:S(2)}, u32[]{:S(2)}) collective-permute-start(bf16[64,8192]{1,0:T(8,128)(2,1)S(1)} %pad_maximum_fusion.refs_0_), channel_id=1, source_target_pairs={{0,6},{2,0},{4,2},{6,4},{1,7},{3,1},{5,3},{7,5},{8,14},{10,8},{12,... | collective-permute-start | bytes 3145736 | tf_op jit(solution)/shard_map/ppermute | solution.py:393
  51.7 17.9 %collective-permute-start.12 = (bf16[1024,128]{1,0:T(8,128)(2,1)}, bf16[1024,128]{1,0:T(8,128)(2,1)S(1)}, u32[]{:S(2)}, u32[]{:S(2)}) collective-permute-start(bf16[1024,128]{1,0:T(8,128)(2,1)} %copy-done.17), channel_id=1, source_target_pairs={{0,32},{32,64},{64,96},{96,0},{1,33},{33,65},{65,97},{97,1},{2,34}... | collective-permute-start | bytes 786440 | tf_op jit(solution)/shard_map/ppermute | solution.py:393
  53.2 3.4 %copy-start = (bf16[8192,512]{1,0:T(8,128)(2,1)S(1)}, bf16[8192,512]{1,0:T(8,128)(2,1)}, u32[]{:S(2)}) copy-start(bf16[8192,512]{1,0:T(8,128)(2,1)} %refs_2_) | copy-start | bytes 25165828
  56.6 1.6 copy-start.4
  68.8 0.8 copy-start.18
  69.6 8.8 %copy-start.13 = (bf16[1024,128]{1,0:T(8,128)(2,1)S(1)}, bf16[1024,128]{1,0:T(8,128)(2,1)}, u32[]{:S(2)}) copy-start(bf16[1024,128]{1,0:T(8,128)(2,1)} %copy-done.12) | copy-start | bytes 786436
  69.6 3.5 %copy-start.20 = (bf16[1024,128]{1,0:T(8,128)(2,1)}, bf16[1024,128]{1,0:T(8,128)(2,1)S(1)}, u32[]{:S(2)}) copy-start(bf16[1024,128]{1,0:T(8,128)(2,1)S(1)} %collective-permute-done.12) | copy-start | bytes 786436
  73.1 39.0 %collective-permute-start.21 = (bf16[512,8192]{1,0:T(8,128)(2,1)}, bf16[512,8192]{1,0:T(8,128)(2,1)}, u32[]{:S(2)}, u32[]{:S(2)}) collective-permute-start(bf16[512,8192]{1,0:T(8,128)(2,1)} %mine_ref.2), channel_id=1, source_target_pairs={{0,1},{1,0},{2,3},{3,2},{4,5},{5,4},{6,7},{7,6},{8,9},{9,8},{10,11... | collective-permute-start | bytes 25165832 | tf_op jit(solution)/shard_map/ppermute | solution.py:388
  73.3 7.7 %copy-start.16 = (bf16[1024,128]{1,0:T(8,128)(2,1)S(1)}, bf16[1024,128]{1,0:T(8,128)(2,1)}, u32[]{:S(2)}) copy-start(bf16[1024,128]{1,0:T(8,128)(2,1)} %copy-done.15) | copy-start | bytes 786436
  73.3 9.4 %copy-start.5 = (bf16[8192,128]{1,0:T(8,128)(2,1)S(1)}, bf16[8192,128]{1,0:T(8,128)(2,1)}, u32[]{:S(2)}) copy-start(bf16[8192,128]{1,0:T(8,128)(2,1)} %copy-done.3) | copy-start | bytes 6291460
  75.1 20.6 %collective-permute-start.13 = (bf16[32,8192]{1,0:T(8,128)(2,1)S(1)}, bf16[32,8192]{1,0:T(8,128)(2,1)S(1)}, u32[]{:S(2)}, u32[]{:S(2)}) collective-permute-start(bf16[32,8192]{1,0:T(8,128)(2,1)S(1)} %get-tuple-element.109), channel_id=1, source_target_pairs={{0,2},{2,4},{4,6},{6,0},{1,3},{3,5},{5,7},{7,1},{8,10},{10,12},{12... | collective-permute-start | bytes 1572872 | tf_op jit(solution)/shard_map/ppermute | solution.py:393
  76.0 19.7 %collective-permute-start.14 = (bf16[32,8192]{1,0:T(8,128)(2,1)S(1)}, bf16[32,8192]{1,0:T(8,128)(2,1)S(1)}, u32[]{:S(2)}, u32[]{:S(2)}) collective-permute-start(bf16[32,8192]{1,0:T(8,128)(2,1)S(1)} %get-tuple-element.110), channel_id=1, source_target_pairs={{0,6},{2,0},{4,2},{6,4},{1,7},{3,1},{5,3},{7,5},{8,14},{10,8},{12,... | collective-permute-start | bytes 1572872 | tf_op jit(solution)/shard_map/ppermute | solution.py:393
  79.4 16.2 %collective-permute-start.15 = (bf16[1024,128]{1,0:T(8,128)(2,1)S(1)}, bf16[1024,128]{1,0:T(8,128)(2,1)S(1)}, u32[]{:S(2)}, u32[]{:S(2)}) collective-permute-start(bf16[1024,128]{1,0:T(8,128)(2,1)S(1)} %add_convert_fusion), channel_id=1, source_target_pairs={{0,32},{32,64},{64,96},{96,0},{1,33},{33,65},{65,97},{97,1},{2,34}... | collective-permute-start | bytes 786440 | tf_op jit(solution)/shard_map/ppermute | solution.py:393
  81.0 14.7 %collective-permute-start.16 = (bf16[1024,128]{1,0:T(8,128)(2,1)S(1)}, bf16[1024,128]{1,0:T(8,128)(2,1)S(1)}, u32[]{:S(2)}, u32[]{:S(2)}) collective-permute-start(bf16[1024,128]{1,0:T(8,128)(2,1)S(1)} %copy-done.16), channel_id=1, source_target_pairs={{0,96},{32,0},{64,32},{96,64},{1,97},{33,1},{65,33},{97,65},{2,98}... | collective-permute-start | bytes 786440 | tf_op jit(solution)/shard_map/ppermute | solution.py:393
  82.7 3.4 %copy-start.1 = (bf16[8192,512]{1,0:T(8,128)(2,1)S(1)}, bf16[8192,512]{1,0:T(8,128)(2,1)}, u32[]{:S(2)}) copy-start(bf16[8192,512]{1,0:T(8,128)(2,1)} %refs_2_) | copy-start | bytes 25165828
  95.6 11.0 %collective-permute-start.17 = (bf16[256,256]{1,0:T(8,128)(2,1)S(1)}, bf16[256,256]{1,0:T(8,128)(2,1)S(1)}, u32[]{:S(2)}, u32[]{:S(2)}) collective-permute-start(bf16[256,256]{1,0:T(8,128)(2,1)S(1)} %get-tuple-element.121.refs_3_), channel_id=1, source_target_pairs={{0,1},{1,0},{2,3},{3,2},{4,5},{5,4},{6,7},{7,6},{8,9},{9,8},{10,11... | collective-permute-start | bytes 393224 | tf_op jit(solution)/shard_map/ppermute | solution.py:388
  95.7 9.0 %copy-start.10 = (bf16[1024,128]{1,0:T(8,128)(2,1)S(1)}, bf16[1024,128]{1,0:T(8,128)(2,1)}, u32[]{:S(2)}) copy-start(bf16[1024,128]{1,0:T(8,128)(2,1)} %copy-done.9) | copy-start | bytes 786436
  95.7 10.9 %copy-start.19 = (bf16[256,1024]{1,0:T(8,128)(2,1)S(1)}, bf16[256,1024]{1,0:T(8,128)(2,1)}, u32[]{:S(2)}) copy-start(bf16[256,1024]{1,0:T(8,128)(2,1)} %copy-done.18) | copy-start | bytes 1572868
  95.7 10.9 %collective-permute-start.18 = (bf16[192,256]{1,0:T(8,128)(2,1)S(1)}, bf16[192,256]{1,0:T(8,128)(2,1)S(1)}, u32[]{:S(2)}, u32[]{:S(2)}) collective-permute-start(bf16[192,256]{1,0:T(8,128)(2,1)S(1)} %get-tuple-element.122.refs_4_), channel_id=1, source_target_pairs={{0,1},{1,0},{2,3},{3,2},{4,5},{5,4},{6,7},{7,6},{8,9},{9,8},{10,11... | collective-permute-start | bytes 294920 | tf_op jit(solution)/shard_map/ppermute | solution.py:388
  104.5 2.1 %collective-permute-start.19 = (bf16[64,256]{1,0:T(8,128)(2,1)S(1)}, bf16[64,256]{1,0:T(8,128)(2,1)S(1)}, u32[]{:S(2)}, u32[]{:S(2)}) collective-permute-start(bf16[64,256]{1,0:T(8,128)(2,1)S(1)} %get-tuple-element.123.refs_5_), channel_id=1, source_target_pairs={{0,1},{1,0},{2,3},{3,2},{4,5},{5,4},{6,7},{7,6},{8,9},{9,8},{10,11... | collective-permute-start | bytes 98312 | tf_op jit(solution)/shard_map/ppermute | solution.py:388
  104.8 7.3 %collective-permute-start.20 = (bf16[512,128]{1,0:T(8,128)(2,1)S(1)}, bf16[512,128]{1,0:T(8,128)(2,1)S(1)}, u32[]{:S(2)}, u32[]{:S(2)}) collective-permute-start(bf16[512,128]{1,0:T(8,128)(2,1)S(1)} %add_convert_fusion.1), channel_id=1, source_target_pairs={{0,16},{16,0},{1,17},{17,1},{2,18},{18,2},{3,19},{19,3},{4,20},{20... | collective-permute-start | bytes 393224 | tf_op jit(solution)/shard_map/ppermute | solution.py:388
  112.1 12.7 %copy-start.11 = (f32[512,128]{1,0:T(8,128)S(1)}, f32[512,128]{1,0:T(8,128)}, u32[]{:S(2)}) copy-start(f32[512,128]{1,0:T(8,128)} %refs_4_.3) | copy-start | bytes 786436
  121.4 15.6 %collective-permute-start.22 = (bf16[32,8192]{1,0:T(8,128)(2,1)S(1)}, bf16[32,8192]{1,0:T(8,128)(2,1)S(1)}, u32[]{:S(2)}, u32[]{:S(2)}) collective-permute-start(bf16[32,8192]{1,0:T(8,128)(2,1)S(1)} %get-tuple-element.131), channel_id=1, source_target_pairs={{0,2},{2,4},{4,6},{6,0},{1,3},{3,5},{5,7},{7,1},{8,10},{10,12},{12... | collective-permute-start | bytes 1572872 | tf_op jit(solution)/shard_map/ppermute | solution.py:393
  121.5 15.5 %collective-permute-start.23 = (bf16[32,8192]{1,0:T(8,128)(2,1)S(1)}, bf16[32,8192]{1,0:T(8,128)(2,1)S(1)}, u32[]{:S(2)}, u32[]{:S(2)}) collective-permute-start(bf16[32,8192]{1,0:T(8,128)(2,1)S(1)} %get-tuple-element.133), channel_id=1, source_target_pairs={{0,6},{2,0},{4,2},{6,4},{1,7},{3,1},{5,3},{7,5},{8,14},{10,8},{12,... | collective-permute-start | bytes 1572872 | tf_op jit(solution)/shard_map/ppermute | solution.py:393
  126.3 10.7 %collective-permute-start.24 = (bf16[512,128]{1,0:T(8,128)(2,1)S(1)}, bf16[512,128]{1,0:T(8,128)(2,1)S(1)}, u32[]{:S(2)}, u32[]{:S(2)}) collective-permute-start(bf16[512,128]{1,0:T(8,128)(2,1)S(1)} %get-tuple-element.137), channel_id=1, source_target_pairs={{0,16},{16,0},{1,17},{17,1},{2,18},{18,2},{3,19},{19,3},{4,20},{20... | collective-permute-start | bytes 393224 | tf_op jit(solution)/shard_map/ppermute | solution.py:388
  137.3 27.4 %collective-permute-start.25 = (bf16[64,8192]{1,0:T(8,128)(2,1)S(1)}, bf16[64,8192]{1,0:T(8,128)(2,1)S(1)}, u32[]{:S(2)}, u32[]{:S(2)}) collective-permute-start(bf16[64,8192]{1,0:T(8,128)(2,1)S(1)} %get-tuple-element.141), channel_id=1, source_target_pairs={{0,2},{2,4},{4,6},{6,0},{1,3},{3,5},{5,7},{7,1},{8,10},{10,12},{12... | collective-permute-start | bytes 3145736 | tf_op jit(solution)/shard_map/ppermute | solution.py:393
  137.4 27.3 %collective-permute-start.26 = (bf16[64,8192]{1,0:T(8,128)(2,1)S(1)}, bf16[64,8192]{1,0:T(8,128)(2,1)S(1)}, u32[]{:S(2)}, u32[]{:S(2)}) collective-permute-start(bf16[64,8192]{1,0:T(8,128)(2,1)S(1)} %get-tuple-element.142), channel_id=1, source_target_pairs={{0,6},{2,0},{4,2},{6,4},{1,7},{3,1},{5,3},{7,5},{8,14},{10,8},{12,... | collective-permute-start | bytes 3145736 | tf_op jit(solution)/shard_map/ppermute | solution.py:393
  140.6 14.0 %collective-permute-start.27 = (bf16[1024,128]{1,0:T(8,128)(2,1)S(1)}, bf16[1024,128]{1,0:T(8,128)(2,1)S(1)}, u32[]{:S(2)}, u32[]{:S(2)}) collective-permute-start(bf16[1024,128]{1,0:T(8,128)(2,1)S(1)} %pad_maximum_fusion.1.refs_0_), channel_id=1, source_target_pairs={{0,32},{32,64},{64,96},{96,0},{1,33},{33,65},{65,97},{97,1},{2,34}... | collective-permute-start | bytes 786440 | tf_op jit(solution)/shard_map/ppermute | solution.py:393
  151.3 22.9 %collective-permute-start.32 = (bf16[32,8192]{1,0:T(8,128)(2,1)S(1)}, bf16[32,8192]{1,0:T(8,128)(2,1)S(1)}, u32[]{:S(2)}, u32[]{:S(2)}) collective-permute-start(bf16[32,8192]{1,0:T(8,128)(2,1)S(1)} %get-tuple-element.156), channel_id=1, source_target_pairs={{0,2},{2,4},{4,6},{6,0},{1,3},{3,5},{5,7},{7,1},{8,10},{10,12},{12... | collective-permute-start | bytes 1572872 | tf_op jit(solution)/shard_map/ppermute | solution.py:393
  151.4 22.8 %collective-permute-start.33 = (bf16[32,8192]{1,0:T(8,128)(2,1)S(1)}, bf16[32,8192]{1,0:T(8,128)(2,1)S(1)}, u32[]{:S(2)}, u32[]{:S(2)}) collective-permute-start(bf16[32,8192]{1,0:T(8,128)(2,1)S(1)} %get-tuple-element.158), channel_id=1, source_target_pairs={{0,6},{2,0},{4,2},{6,4},{1,7},{3,1},{5,3},{7,5},{8,14},{10,8},{12,... | collective-permute-start | bytes 1572872 | tf_op jit(solution)/shard_map/ppermute | solution.py:393
  154.6 6.8 %collective-permute-start.28 = (bf16[1024,128]{1,0:T(8,128)(2,1)S(1)}, bf16[1024,128]{1,0:T(8,128)(2,1)S(1)}, u32[]{:S(2)}, u32[]{:S(2)}) collective-permute-start(bf16[1024,128]{1,0:T(8,128)(2,1)S(1)} %pad_maximum_fusion.1.refs_0_), channel_id=1, source_target_pairs={{0,96},{32,0},{64,32},{96,64},{1,97},{33,1},{65,33},{97,65},{2,98}... | collective-permute-start | bytes 786440 | tf_op jit(solution)/shard_map/ppermute | solution.py:393
  165.0 23.6 %copy-start.8 = (bf16[512,1024]{1,0:T(8,128)(2,1)S(1)}, bf16[512,1024]{1,0:T(8,128)(2,1)}, u32[]{:S(2)}) copy-start(bf16[512,1024]{1,0:T(8,128)(2,1)} %params_ref.1) | copy-start | bytes 3145732
  165.0 20.3 %collective-permute-start.29 = (bf16[32,8192]{1,0:T(8,128)(2,1)S(1)}, bf16[32,8192]{1,0:T(8,128)(2,1)S(1)}, u32[]{:S(2)}, u32[]{:S(2)}) collective-permute-start(bf16[32,8192]{1,0:T(8,128)(2,1)S(1)} %get-tuple-element.151), channel_id=1, source_target_pairs={{0,16},{16,8},{8,24},{24,0},{1,17},{17,9},{9,25},{25,1},{2,18},{18... | collective-permute-start | bytes 1572872 | tf_op jit(solution)/shard_map/ppermute | solution.py:393
  166.4 19.0 %collective-permute-start.30 = (bf16[32,8192]{1,0:T(8,128)(2,1)S(1)}, bf16[32,8192]{1,0:T(8,128)(2,1)S(1)}, u32[]{:S(2)}, u32[]{:S(2)}) collective-permute-start(bf16[32,8192]{1,0:T(8,128)(2,1)S(1)} %get-tuple-element.152), channel_id=1, source_target_pairs={{0,24},{16,0},{8,16},{24,8},{1,25},{17,1},{9,17},{25,9},{2,26},{18... | collective-permute-start | bytes 1572872 | tf_op jit(solution)/shard_map/ppermute | solution.py:393
  174.5 24.8 %collective-permute-start.34 = (bf16[64,8192]{1,0:T(8,128)(2,1)S(1)}, bf16[64,8192]{1,0:T(8,128)(2,1)S(1)}, u32[]{:S(2)}, u32[]{:S(2)}) collective-permute-start(bf16[64,8192]{1,0:T(8,128)(2,1)S(1)} %get-tuple-element.159), channel_id=1, source_target_pairs={{0,2},{2,4},{4,6},{6,0},{1,3},{3,5},{5,7},{7,1},{8,10},{10,12},{12... | collective-permute-start | bytes 3145736 | tf_op jit(solution)/shard_map/ppermute | solution.py:393
  175.0 24.2 %collective-permute-start.35 = (bf16[64,8192]{1,0:T(8,128)(2,1)S(1)}, bf16[64,8192]{1,0:T(8,128)(2,1)S(1)}, u32[]{:S(2)}, u32[]{:S(2)}) collective-permute-start(bf16[64,8192]{1,0:T(8,128)(2,1)S(1)} %get-tuple-element.160), channel_id=1, source_target_pairs={{0,6},{2,0},{4,2},{6,4},{1,7},{3,1},{5,3},{7,5},{8,14},{10,8},{12,... | collective-permute-start | bytes 3145736 | tf_op jit(solution)/shard_map/ppermute | solution.py:393
  177.8 7.6 %collective-permute-start.31 = (bf16[1024,128]{1,0:T(8,128)(2,1)S(1)}, bf16[1024,128]{1,0:T(8,128)(2,1)S(1)}, u32[]{:S(2)}, u32[]{:S(2)}) collective-permute-start(bf16[1024,128]{1,0:T(8,128)(2,1)S(1)} %collective-permute-done.27.refs_2_), channel_id=1, source_target_pairs={{0,32},{32,64},{64,96},{96,0},{1,33},{33,65},{65,97},{97,1},{2,34}... | collective-permute-start | bytes 786440 | tf_op jit(solution)/shard_map/ppermute | solution.py:393
  185.4 13.9 %collective-permute-start.36 = (bf16[32,8192]{1,0:T(8,128)(2,1)S(1)}, bf16[32,8192]{1,0:T(8,128)(2,1)S(1)}, u32[]{:S(2)}, u32[]{:S(2)}) collective-permute-start(bf16[32,8192]{1,0:T(8,128)(2,1)S(1)} %collective-permute-done.29), channel_id=1, source_target_pairs={{0,16},{16,8},{8,24},{24,0},{1,17},{17,9},{9,25},{25,1},{2,18},{18... | collective-permute-start | bytes 1572872 | tf_op jit(solution)/shard_map/ppermute | solution.py:393
  186.6 12.6 %collective-permute-start.37 = (bf16[32,8192]{1,0:T(8,128)(2,1)S(1)}, bf16[32,8192]{1,0:T(8,128)(2,1)S(1)}, u32[]{:S(2)}, u32[]{:S(2)}) collective-permute-start(bf16[32,8192]{1,0:T(8,128)(2,1)S(1)} %collective-permute-done.30), channel_id=1, source_target_pairs={{0,24},{16,0},{8,16},{24,8},{1,25},{17,1},{9,17},{25,9},{2,26},{18... | collective-permute-start | bytes 1572872 | tf_op jit(solution)/shard_map/ppermute | solution.py:393

commit v2 on v1

--- a/solution.py
+++ b/solution.py
@@ -61,72 +61,107 @@
     )(rows, gain.reshape(1, width))
 
 
-def project_body(core_ref, *refs):
-    blocks, refs = refs[:-7], refs[-7:]
-    qa_ref, qb_ref, ka_ref, kb_ref, query_out, pair_out, total = refs
-    step, steps = pl.program_id(0), pl.num_programs(0)
-    half = qa_ref.shape[1]
-
-    @pl.when(step == 0)
-    def _():
-        total[...] = jnp.zeros_like(total)
-
-    rows = jnp.concatenate([ref[...] for ref in blocks], axis=0)
-    both = jnp.concatenate([ka_ref[...], kb_ref[...]], axis=1)
-    for start, weight in ((0, qa_ref[...]), (half, qb_ref[...]), (2 * half, both)):
-        total[:, start : start + weight.shape[1]] += jnp.dot(
-            rows, weight, preferred_element_type=jnp.float32
-        )
-
-    @pl.when(step == steps - 1)
-    def _():
-        flip = core_ref[0] == 0
-        value = total[...].astype(jnp.bfloat16)
-        query_out[...] = value[:, : 2 * half]
-        left, right = value[:, 2 * half : 2 * half + HEAD], value[:, 2 * half + HEAD :]
-        pair_out[:, :HEAD] = jnp.where(flip, left, right)
-        pair_out[:, HEAD:] = jnp.where(flip, right, left)
+def project_body(tile, core_ref, *refs):
+    blocks, refs = refs[:-12], refs[-12:]
+    weights, (query_out, pair_out, total), held, arrived = refs[:4], refs[4:7], refs[7:11], refs[11]
+    half = weights[0].shape[1]
+    depth = weights[0].shape[0]
+    chunks = arrived.shape[1]
+    chunk = depth // chunks
+    copies = [
+        [
+            pltpu.make_async_copy(
+                weight.at[pl.ds(at * chunk, chunk), :],
+                place.at[pl.ds(at * chunk, chunk), :],
+                arrived.at[kind, at],
+            )
+            for kind, (weight, place) in enumerate(zip(weights, held))
+        ]
+        for at in range(chunks)
+    ]
+    for group in copies:
+        for copy in group:
+            copy.start()
+    total[...] = jnp.zeros_like(total)
+    qa_ref, qb_ref, ka_ref, kb_ref = held
+
+    def step(at, carry):
+        span = pl.ds(pl.multiple_of(at * tile, tile), tile)
+        rows = jnp.concatenate([ref[:, span] for ref in blocks], axis=0)
+        both = jnp.concatenate([ka_ref[span, :], kb_ref[span, :]], axis=1)
+        for start, weight in ((0, qa_ref[span, :]), (half, qb_ref[span, :]), (2 * half, both)):
+            total[:, start : start + weight.shape[1]] += jnp.dot(
+                rows, weight, preferred_element_type=jnp.float32
+            )
+        return carry
+
+    per = chunk // tile
+    for at, group in enumerate(copies):
+        for copy in group:
+            copy.wait()
+        lax.fori_loop(at * per, (at + 1) * per, step, 0)
+    flip = core_ref[0] == 0
+    value = total[...].astype(jnp.bfloat16)
+    query_out[...] = value[:, : 2 * half]
+    left, right = value[:, 2 * half : 2 * half + HEAD], value[:, 2 * half + HEAD :]
+    pair_out[:, :HEAD] = jnp.where(flip, left, right)
+    pair_out[:, HEAD:] = jnp.where(flip, right, left)
 
 
 def project(core, blocks, weights):
     width = blocks[0].shape[1]
-    tile = 1024
     count = sum(block.shape[0] for block in blocks)
     qcols = 2 * weights[0].shape[1]
     kcols = 2 * weights[2].shape[1]
-    smem = pl.BlockSpec(memory_space=pltpu.SMEM)
-    whole = lambda cols: pl.BlockSpec((count, cols), lambda i: (0, 0))
-    return pl.pallas_call(
-        project_body,
-        grid=(width // tile,),
-        in_specs=[smem]
-        + [pl.BlockSpec((block.shape[0], tile), lambda i: (0, i)) for block in blocks]
-        + [pl.BlockSpec((tile, w.shape[1]), lambda i: (i, 0)) for w in weights],
-        out_specs=[whole(qcols), whole(kcols)],
+    vmem = pl.BlockSpec(memory_space=pltpu.VMEM)
+    return pl.pallas_call(
+        functools.partial(project_body, 1024),
+        in_specs=[pl.BlockSpec(memory_space=pltpu.SMEM)]
+        + [vmem] * len(blocks)
+        + [pl.BlockSpec(memory_space=pl.ANY)] * len(weights),
+        out_specs=[vmem, vmem],
         out_shape=[
             jax.ShapeDtypeStruct((count, qcols), jnp.bfloat16),
             jax.ShapeDtypeStruct((count, kcols), jnp.bfloat16),
         ],
-        scratch_shapes=[pltpu.VMEM((count, qcols + kcols), jnp.float32)],
-        compiler_params=params(16),
+        scratch_shapes=[pltpu.VMEM((count, qcols + kcols), jnp.float32)]
+        + [pltpu.VMEM(weight.shape, jnp.bfloat16) for weight in weights]
+        + [pltpu.SemaphoreType.DMA((len(weights), 4))],
+        compiler_params=params(32),
         cost_estimate=cost(
-            2 * 2 * count * width * (qcols + kcols), 2 * width * (count + qcols + kcols)
+            2 * count * width * (qcols + kcols), 2 * width * (count + qcols + kcols)
         ),
         name="project",
     )(core, *blocks, *weights)
 
 
-def attend_body(core_ref, place_ref, *refs):
-    *ins, mixed_ref, query_ref, own_ref, other_ref = refs
+def attend_body(order, core_ref, place_ref, *refs):
+    ins, refs = refs[:-10], refs[-10:]
+    weights, mixed_ref, far_refs = refs[:2], refs[2], refs[3:5]
+    query_ref, own_ref, other_ref, held, arrived = refs[5:]
+    half, width = weights[0].shape
+    chunks = arrived.shape[1]
+    chunk = half // chunks
+    copies = [
+        pltpu.make_async_copy(
+            weight.at[pl.ds(at * chunk, chunk), :],
+            held.at[pl.ds(kind * half + at * chunk, chunk), :],
+            arrived.at[kind, at],
+        )
+        for kind, weight in enumerate(weights)
+        for at in range(chunks)
+    ]
+    for copy in copies:
+        copy.start()
     core = core_ref[0]
     parts = len(ins) // 3
     for kind, whole in enumerate((query_ref, own_ref, other_ref)):
-        slot = 0
+        at = 0
         for part in ins[kind * parts : (kind + 1) * parts]:
             for top in range(0, part.shape[0], ROWS):
-                place = pl.ds(pl.multiple_of(place_ref[slot] * ROWS, ROWS), ROWS)
+                place = pl.ds(pl.multiple_of(place_ref[order[at]] * ROWS, ROWS), ROWS)
                 whole[place, :] = part[top : top + ROWS]
-                slot += 1
+                at += 1
     count, qcols = query_ref.shape
     heads = qcols // HEAD
     block = 2 * ROWS
@@ -177,22 +212,42 @@
                 top = h * block + part * ROWS
                 mixed_ref[place, h * HEAD : (h + 1) * HEAD] = mixed[top : top + ROWS]
 
-
-def attend(core, places, queries, own, other):
+    for copy in copies:
+        copy.wait()
+    rows = mixed_ref[count - ROWS :]
+    tile = 1024
+
+    def far(at, carry):
+        span = pl.ds(pl.multiple_of(at * tile, tile), tile)
+        result = jnp.dot(rows, held[:, span], preferred_element_type=jnp.float32)
+        result = result.astype(jnp.bfloat16)
+        for side, far_ref in enumerate(far_refs):
+            far_ref[:, span] = result[side * ROWS // HALVES : (side + 1) * ROWS // HALVES]
+        return carry
+
+    lax.fori_loop(0, width // tile, far, 0)
+
+
+def attend(core, places, order, queries, own, other, weights):
     count, qcols = sum(q.shape[0] for q in queries), queries[0].shape[1]
     kcols = own[0].shape[1]
     args = [*queries, *own, *other]
     vmem = pl.BlockSpec(memory_space=pltpu.VMEM)
-    return pl.pallas_call(
-        attend_body,
-        in_specs=[pl.BlockSpec(memory_space=pltpu.SMEM)] * 2 + [vmem] * len(args),
-        out_specs=vmem,
-        out_shape=jax.ShapeDtypeStruct((count, qcols), jnp.bfloat16),
-        scratch_shapes=[pltpu.VMEM((count, cols), jnp.bfloat16) for cols in (qcols, kcols, kcols)],
-        compiler_params=params(28),
-        cost_estimate=cost(8 * count * count * qcols, 4 * count * qcols),
+    depth, width = weights[0].shape
+    return pl.pallas_call(
+        functools.partial(attend_body, order),
+        in_specs=[pl.BlockSpec(memory_space=pltpu.SMEM)] * 2
+        + [vmem] * len(args)
+        + [pl.BlockSpec(memory_space=pl.ANY)] * 2,
+        out_specs=[vmem] * 3,
+        out_shape=[jax.ShapeDtypeStruct((count, qcols), jnp.bfloat16)]
+        + [jax.ShapeDtypeStruct((ROWS // HALVES, width), jnp.bfloat16)] * HALVES,
+        scratch_shapes=[pltpu.VMEM((count, cols), jnp.bfloat16) for cols in (qcols, kcols, kcols)]
+        + [pltpu.VMEM((2 * depth, width), jnp.bfloat16), pltpu.SemaphoreType.DMA((2, 4))],
+        compiler_params=params(48),
+        cost_estimate=cost(8 * count * count * qcols, 4 * count * qcols + 4 * depth * width),
         name="attend",
-    )(core, places, *args)
+    )(core, places, *args, *weights)
 
 
 def output_body(first, mixed_ref, mine_ref, theirs_ref, *out_refs):
@@ -226,21 +281,22 @@
     )(mixed, mine, theirs)
 
 
-def pick_body(below_ref, above_ref, first_ref, second_ref):
-    count = first_ref.shape[0]
-    first_ref[...] = below_ref[:count]
-    second_ref[...] = above_ref[count:]
-
-
-def pick(below, above, flops):
-    shape = jax.ShapeDtypeStruct((below.shape[0] // HALVES, below.shape[1]), below.dtype)
-    return pl.pallas_call(
-        pick_body,
-        out_shape=[shape, shape],
+def mark_body(*refs):
+    del refs
+
+
+def mark(*blocks):
+    anywhere = [pl.BlockSpec(memory_space=pl.ANY)] * len(blocks)
+    return pl.pallas_call(
+        mark_body,
+        in_specs=anywhere,
+        out_specs=anywhere,
+        out_shape=[jax.ShapeDtypeStruct(block.shape, block.dtype) for block in blocks],
+        input_output_aliases={at: at for at in range(len(blocks))},
         compiler_params=params(),
-        cost_estimate=cost(flops, 4 * below.size),
-        name="pick",
-    )(below, above)
+        cost_estimate=cost(1e11, 4096),
+        name="mark",
+    )(*blocks)
 
 
 def split_body(*refs):
@@ -434,46 +490,44 @@
     )
     query_theirs = swap(query_weight, "core")
     partner = jnp.concatenate([hop(relay1, Y, 1), hop(relay2, Y, -1)], axis=0)
-    far1, far2 = pick(below, above, 1.5e11)
-    partner = tie(partner, far1, far2)
-    pbelow, pabove = hop(partner, "z", 1), hop(partner, "z", -1)
-    far1, far2 = hop(far1, "z", 1), hop(far2, "z", -1)
+    below, above = mark(below, above)
+    far = hop(below, "z", 1)
+    partner, above, below = wait(partner, above, below)
+    pabove, pbelow = hop(partner, "z", -1), hop(partner, "z", 1)
     weights = [query_weight, query_theirs, kv_weight, kv_theirs]
-    query_a, pair_a = project(core, [block, above, below, far1, far2], weights)
-    x2 = hop(tie(at2, far1), "x", 1)
-    pbelow, pabove, query_a, pair_a, x2, at1, at3, out_weight = wait(
-        pbelow, pabove, query_a, pair_a, x2, at1, at3, out_weight
-    )
-    pfar1, pfar2 = pick(pbelow, pabove, 1e8)
-    pfar1, pfar2 = hop(pfar1, "z", 1), hop(pfar2, "z", -1)
-    passed, x3 = hop(add(at1, x2), "x", 1), hop(at3, "x", -1)
-    query_m, pair_m = project(core, [partner, pabove, pbelow], weights)
+    query_a, pair_a = project(core, [block, above, below, partner], weights)
+    at2, at3 = wait(at2, at3, partner)[:2]
+    x2, x3 = hop(at2, "x", 1), hop(at3, "x", -1)
+    pabove, far, query_a, pair_a, x2, x3, at1, out_weight = wait(
+        pabove, far, query_a, pair_a, x2, x3, at1, out_weight
+    )
+    pfar = hop(pabove, "z", -1)
     out_theirs = swap(out_weight, "core")
-    pfar1, pfar2, query_m, pair_m, passed, x3, at0 = wait(
-        pfar1, pfar2, query_m, pair_m, passed, x3, at0
-    )
+    query_m, pair_m = project(core, [far, pabove], weights)
+    passed = hop(add(at1, x2), "x", 1)
     other_a, other_m = swap(pair_a, "core"), swap(pair_m, "core")
-    query_l, pair_l = project(core, [pfar1, pfar2], weights)
+    pbelow, pfar, passed, query_m = wait(pbelow, pfar, passed, query_m)
+    query_l, pair_l = project(core, [pbelow, pfar], weights)
     other_l = swap(pair_l, "core")
-    mine = (at0, passed, x3)
-    count = momentum.shape[0]
-    theirs = swap(add(*(part[count:] for part in mine)), "ylo")
-    mixed = attend(
+    mixed, up1, down2 = attend(
         core,
         places,
+        (0, 1, 2, 4, 3, 5, 6, 7),
         (query_a, query_m, query_l),
         (pair_a, pair_m, pair_l),
         (other_a, other_m, other_l),
-    )
-    mixed, theirs, out_theirs = wait(mixed, theirs, out_theirs)
+        (out_weight, out_theirs),
+    )
 
     half = ROWS // HALVES
     theirs_at = len(RING) * ROWS
-    up1, down2 = output(mixed, out_weight, out_theirs, theirs_at + 3 * ROWS, [half] * HALVES)
     up1, down2 = hop(up1, "z", 1), hop(down2, "z", -1)
+    mine = (at0, passed, x3)
+    count = momentum.shape[0]
+    q0, qup, qdown = output(mixed, out_weight, out_theirs, theirs_at, [ROWS] * 3)
+    theirs = swap(tie(add(*(part[count:] for part in mine)), q0), "ylo")
     new_momentum, rebuilt = outer(mine, theirs, momentum, hadamard_table(HEAD), replicas)
     beside = swap(rebuilt, "ylo")
-    q0, qup, qdown = output(mixed, out_weight, out_theirs, theirs_at, [ROWS] * 3)
     up, down = sums((qup, (up1, 0)), (qdown, (down2, half)))
     both = jnp.concatenate([rebuilt, beside], axis=0)
     up, down, both, mixed = wait(up, down, both, mixed)

time: 202 us -> 202 us (level)
  waiting for transfers between devices: 52.8 us -> 61.4 us
  Pallas kernels: 76.3 us -> 68.8 us
  starting transfers between devices: 51.7 us -> 47.1 us
  local copies, waits for them, and re-layouts: 16.4 us -> 19.6 us
    ppermute x8, waiting for transfers between devices: 0.02 us -> 9.73 us  [swap(): return lax.ppermute(block, axis, [(0, 1), (1, 0)])]
    pallas_call x3 -> x2, Pallas kernels: 29.6 us -> 20.3 us  [output(): pl.pallas_call(functools.partial(output_body, first), grid=(width // tile...]
    unnamed x43 -> x41, local copies, waits for them, and re-layouts: 16.3 us -> 19.4 us
    ppermute x30 -> x28, starting transfers between devices: 48.2 us -> 45.6 us  [hop(): lax.ppermute(block, axis, [(at[i], at[(i + way) % 4]) for i in range(4)])]
    ppermute x8, starting transfers between devices: 3.51 us -> 1.46 us  [swap(): return lax.ppermute(block, axis, [(0, 1), (1, 0)])]
    ppermute x30 -> x28, waiting for transfers between devices: 52.8 us -> 51.7 us  [hop(): lax.ppermute(block, axis, [(at[i], at[(i + way) % 4]) for i in range(4)])]
    pallas_call x6 -> x5, Pallas kernels: 38 us -> 38.4 us  [the longest x3 26.1 us: project(): pl.pallas_call(functools.partial(project_body, 1024), in_specs=[pl.BlockS...]
  transfers between devices with their start and end apart: 38 -> 36, of which waited for: 11 -> 13; matrix products, arithmetic and copies ran while one was open for 2% -> 2% of each run, Pallas kernels for 32% -> 26%
where the time goes in v2:
time: 202 us; the launch traced here: 201 us
  Pallas kernels  68.8 us (34%)
  waiting for transfers between devices  61.4 us (30%)
  starting transfers between devices  47.1 us (23%)
  local copies, waits for them, and re-layouts  19.6 us (10%)
  other arithmetic  2.94 us (1%)
    ppermute x28, waiting for transfers between devices, hop(): lax.ppermute(block, axis, [(at[i], at[(i + way) % 4]) for i in range(4)])  51.7 us
    ppermute x28, starting transfers between devices, hop(): lax.ppermute(block, axis, [(at[i], at[(i + way) % 4]) for i in range(4)])  45.6 us
    pallas_call x3, Pallas kernels, project(): pl.pallas_call(functools.partial(project_body, 1024), in_specs=[pl.BlockS...  26.1 us
    pallas_call x2, Pallas kernels, output(): pl.pallas_call(functools.partial(output_body, first), grid=(width // tile...  20.3 us
    unnamed x41, local copies, waits for them, and re-layouts  19.4 us
    pallas_call x1, Pallas kernels, attend(): pl.pallas_call(functools.partial(attend_body, order), in_specs=[pl.BlockS...  12.3 us
    ppermute x8, waiting for transfers between devices, swap(): return lax.ppermute(block, axis, [(0, 1), (1, 0)])  9.73 us
  transfers between devices with their start and end apart: 36, of which 13 were waited for; matrix products, arithmetic and copies ran while one was open for 2% of the time, Pallas kernels for 26%

profile of v2, /device:TPU:0, one launch (start us, length us, event | category | flops | bytes accessed | tf_op | source)
XLA Modules:
  0.0 200.8 jit_solution(726201232280141400)
XLA Ops:
  0.6 1.2 copy-done.9
  1.9 0.8 copy-done.17
  2.6 1.6 normalize.1
  4.2 2.0 collective-permute-start.5
  6.2 2.2 %collective-permute-start.6 = (bf16[64,8192]{1,0:T(8,128)(2,1)S(1)}, bf16[64,8192]{1,0:T(8,128)(2,1)}, u32[]{:S(2)}, u32[]{:S(2)}) collective-permute-start(bf16[64,8192]{1,0:T(8,128)(2,1)S(1)} %get-tuple-element.83.refs_0_), channel_id=1, source_target_pairs={{0,6},{2,0},{4,2},{6,4},{1,7},{3,1},{5,3},{7,5},{8,14},{10,8},{12,... | collective-permute-start | bytes 3145736 | tf_op jit(solution)/shard_map/ppermute | solution.py:449
  8.4 1.6 collective-permute-start
  10.0 1.7 collective-permute-start.1
  11.7 0.8 copy.14
  12.6 1.2 copy-done.8
  13.8 1.9 terms.1
  15.7 0.7 copy-done.11
  16.4 0.7 copy-done.16
  17.1 0.7 copy-done.18
  17.8 6.2 %collective-permute-done = bf16[32,8192]{1,0:T(8,128)(2,1)} collective-permute-done((bf16[32,8192]{1,0:T(8,128)(2,1)}, bf16[32,8192]{1,0:T(8,128)(2,1)}, u32[]{:S(2)}, u32[]{:S(2)}) %collective-permute-start) | collective-permute-done | bytes 524320 | tf_op jit(solution)/shard_map/ppermute | solution.py:449
  24.0 1.3 copy-done.3
  25.4 2.9 %collective-permute-start.4 = (bf16[32,8192]{1,0:T(8,128)(2,1)}, bf16[32,8192]{1,0:T(8,128)(2,1)S(1)}, u32[]{:S(2)}, u32[]{:S(2)}) collective-permute-start(bf16[32,8192]{1,0:T(8,128)(2,1)} %collective-permute-done.1), channel_id=1, source_target_pairs={{0,24},{16,0},{8,16},{24,8},{1,25},{17,1},{9,17},{25,9},{2,26},{18... | collective-permute-start | bytes 1572872 | tf_op jit(solution)/shard_map/ppermute | solution.py:449
  28.3 4.0 %collective-permute-done.5.refs_0_ = bf16[64,8192]{1,0:T(8,128)(2,1)} collective-permute-done((bf16[64,8192]{1,0:T(8,128)(2,1)S(1)}, bf16[64,8192]{1,0:T(8,128)(2,1)}, u32[]{:S(2)}, u32[]{:S(2)}) %collective-permute-start.5) | collective-permute-done | bytes 1048608 | tf_op jit(solution)/shard_map/ppermute | solution.py:449
  32.3 1.3 collective-permute-start.8
  33.6 5.5 %collective-permute-done.4 = bf16[32,8192]{1,0:T(8,128)(2,1)S(1)} collective-permute-done((bf16[32,8192]{1,0:T(8,128)(2,1)}, bf16[32,8192]{1,0:T(8,128)(2,1)S(1)}, u32[]{:S(2)}, u32[]{:S(2)}) %collective-permute-start.4) | collective-permute-done | bytes 524320 | tf_op jit(solution)/shard_map/ppermute | solution.py:449
  39.0 3.3 %collective-permute-done.3 = bf16[32,8192]{1,0:T(8,128)(2,1)S(1)} collective-permute-done((bf16[32,8192]{1,0:T(8,128)(2,1)}, bf16[32,8192]{1,0:T(8,128)(2,1)S(1)}, u32[]{:S(2)}, u32[]{:S(2)}) %collective-permute-start.3) | collective-permute-done | bytes 524320 | tf_op jit(solution)/shard_map/ppermute | solution.py:449
  42.4 1.6 collective-permute-start.7
  44.0 1.5 collective-permute-start.10
  45.5 1.7 collective-permute-start.11
  47.2 3.4 %copy-done = bf16[8192,512]{1,0:T(8,128)(2,1)S(1)} copy-done((bf16[8192,512]{1,0:T(8,128)(2,1)S(1)}, bf16[8192,512]{1,0:T(8,128)(2,1)}, u32[]{:S(2)}) %copy-start) | copy-done | bytes 8388632
  50.6 1.6 copy-done.4
  52.2 1.2 copy-done.7
  53.4 10.5 %project.3 = (bf16[256,1024]{1,0:T(8,128)(2,1)S(1)}, bf16[256,256]{1,0:T(8,128)(2,1)S(1)}) custom-call(s32[1]{0:T(128)} %bitcast.core_ref, bf16[64,8192]{1,0:T(8,128)(2,1)S(1)} %copy-done.7, bf16[64,8192]{1,0:T(8,128)(2,1)} %get-tuple-element.95.refs_1_, bf16[64,8192]{1,0:T(8,128)(2,1)} %get-tuple-element.96.refs_2_, ...), custom_call_target="tpu_custom_call" | custom-call | flops 5368709120 | bytes 25165824 | tf_op jit(solution)/shard_map/project/pallas_call | solution.py:117
  63.9 0.8 copy-done.13
  64.7 0.9 collective-permute-done.7.refs_1_
  65.6 3.2 %collective-permute-start.13 = (bf16[64,8192]{1,0:T(8,128)(2,1)}, bf16[64,8192]{1,0:T(8,128)(2,1)}, u32[]{:S(2)}, u32[]{:S(2)}) collective-permute-start(bf16[64,8192]{1,0:T(8,128)(2,1)} %collective-permute-done.7.refs_1_), channel_id=1, source_target_pairs={{0,6},{2,0},{4,2},{6,4},{1,7},{3,1},{5,3},{7,5},{8,14},{10,8},{12,... | collective-permute-start | bytes 3145736 | tf_op jit(solution)/shard_map/ppermute | solution.py:449
  68.9 1.8 add_convert_fusion
  70.7 1.5 collective-permute-start.14
  72.5 3.4 %copy-done.1 = bf16[8192,512]{1,0:T(8,128)(2,1)S(1)} copy-done((bf16[8192,512]{1,0:T(8,128)(2,1)S(1)}, bf16[8192,512]{1,0:T(8,128)(2,1)}, u32[]{:S(2)}) %copy-start.1) | copy-done | bytes 8388632
  75.9 1.6 copy-done.5
  77.5 7.7 %project.4 = (bf16[128,1024]{1,0:T(8,128)(2,1)S(1)}, bf16[128,256]{1,0:T(8,128)(2,1)S(1)}) custom-call(s32[1]{0:T(128)} %bitcast.core_ref, bf16[64,8192]{1,0:T(8,128)(2,1)} %collective-permute-done.8.refs_0_, bf16[64,8192]{1,0:T(8,128)(2,1)} %collective-permute-done.7.refs_1_, bf16[8192,512]{1,0:T(8,128)(2,1)S(1)} %copy-done.1, ...), custom_call_target="tpu_custom_call" | custom-call | flops 2684354560 | bytes 23068672 | tf_op jit(solution)/shard_map/project/pallas_call | solution.py:117
  85.3 7.3 %collective-permute-done.12.refs_0_ = bf16[64,8192]{1,0:T(8,128)(2,1)} collective-permute-done((bf16[64,8192]{1,0:T(8,128)(2,1)S(1)}, bf16[64,8192]{1,0:T(8,128)(2,1)}, u32[]{:S(2)}, u32[]{:S(2)}) %collective-permute-start.12) | collective-permute-done | bytes 1048608 | tf_op jit(solution)/shard_map/ppermute | solution.py:449
  92.6 7.8 %project.5 = (bf16[128,1024]{1,0:T(8,128)(2,1)S(1)}, bf16[128,256]{1,0:T(8,128)(2,1)S(1)}) custom-call(s32[1]{0:T(128)} %bitcast.core_ref, bf16[64,8192]{1,0:T(8,128)(2,1)} %collective-permute-done.12.refs_0_, bf16[64,8192]{1,0:T(8,128)(2,1)} %collective-permute-done.13.refs_1_, bf16[8192,512]{1,0:T(8,128)(2,1)S(1)} %copy-done.1, ...), custom_call_target="tpu_custom_call" | custom-call | flops 2684354560 | bytes 23068672 | tf_op jit(solution)/shard_map/project/pallas_call | solution.py:117
  100.4 0.6 collective-permute-start.17
  101.0 1.0 add_convert_fusion.1
  102.0 12.3 %attend.1 = (bf16[512,1024]{1,0:T(8,128)(2,1)S(1)}, bf16[32,8192]{1,0:T(8,128)(2,1)S(1)}, bf16[32,8192]{1,0:T(8,128)(2,1)S(1)}) custom-call(s32[1]{0:T(128)} %bitcast.core_ref, s32[16]{0:T(128)S(1)} %concatenate.9.place_ref, bf16[256,1024]{1,0:T(8,128)(2,1)S(1)} %copy-done.14, bf16[128,1024]{1,0:T(8,128)(2,1)S(1)} %get-tuple-element.112.refs_1_, ...), custom_call_target="tpu_custom_call" | custom-call | flops 2147483648 | bytes 18874368 | tf_op jit(solution)/shard_map/attend/pallas_call | solution.py:237
  114.3 0.5 collective-permute-start.19
  114.8 2.8 %collective-permute-start.20 = (bf16[32,8192]{1,0:T(8,128)(2,1)S(1)}, bf16[32,8192]{1,0:T(8,128)(2,1)S(1)}, u32[]{:S(2)}, u32[]{:S(2)}) collective-permute-start(bf16[32,8192]{1,0:T(8,128)(2,1)S(1)} %get-tuple-element.124), channel_id=1, source_target_pairs={{0,6},{2,0},{4,2},{6,4},{1,7},{3,1},{5,3},{7,5},{8,14},{10,8},{12,... | collective-permute-start | bytes 1572872 | tf_op jit(solution)/shard_map/ppermute | solution.py:449
  117.6 9.9 %output.2 = (bf16[64,8192]{1,0:T(8,128)(2,1)S(1)}, bf16[64,8192]{1,0:T(8,128)(2,1)S(1)}, bf16[64,8192]{1,0:T(8,128)(2,1)S(1)}) custom-call(bf16[512,1024]{1,0:T(8,128)(2,1)S(1)} %get-tuple-element.133.mixed_ref, bf16[512,8192]{1,0:T(8,128)(2,1)} %mine_ref.1, bf16[512,8192]{1,0:T(8,128)(2,1)} %collective-permute-done.18.refs_10_.theirs_ref), custom_call_target="tpu_custom_call" | custom-call | flops 3221225472 | bytes 19922944 | tf_op jit(solution)/shard_map/output/pallas_call | solution.py:272
  127.9 5.0 %collective-permute-done.21.refs_3_ = bf16[512,128]{1,0:T(8,128)(2,1)S(1)} collective-permute-done((bf16[512,128]{1,0:T(8,128)(2,1)S(1)}, bf16[512,128]{1,0:T(8,128)(2,1)S(1)}, u32[]{:S(2)}, u32[]{:S(2)}) %collective-permute-start.21) | collective-permute-done | bytes 131104 | tf_op jit(solution)/shard_map/ppermute | solution.py:444
  132.9 2.4 %outer.1 = (f32[512,128]{1,0:T(8,128)}, bf16[512,128]{1,0:T(8,128)(2,1)S(1)}) custom-call(bf16[1024,128]{1,0:T(8,128)(2,1)S(1)} %copy-done.12, bf16[1024,128]{1,0:T(8,128)(2,1)} %collective-permute-done.14.refs_1_, bf16[1024,128]{1,0:T(8,128)(2,1)S(1)} %collective-permute-done.11.refs_2_, bf16[512,128]{1,0:T(8,128)(2,1)S(1)} %collective-permute-done.21.refs_3_, ...), custom_call_target="tpu_custom_call" | custom-call | flops 335544320 | bytes 786432 | tf_op jit(solution)/shard_map/outer/pallas_call | solution.py:407
  135.7 4.7 %collective-permute-done.22 = bf16[512,128]{1,0:T(8,128)(2,1)S(1)} collective-permute-done((bf16[512,128]{1,0:T(8,128)(2,1)S(1)}, bf16[512,128]{1,0:T(8,128)(2,1)S(1)}, u32[]{:S(2)}, u32[]{:S(2)}) %collective-permute-start.22) | collective-permute-done | bytes 131104 | tf_op jit(solution)/shard_map/ppermute | solution.py:444
  140.8 3.2 %collective-permute-start.24 = (bf16[64,8192]{1,0:T(8,128)(2,1)S(1)}, bf16[64,8192]{1,0:T(8,128)(2,1)S(1)}, u32[]{:S(2)}, u32[]{:S(2)}) collective-permute-start(bf16[64,8192]{1,0:T(8,128)(2,1)S(1)} %get-tuple-element.137), channel_id=1, source_target_pairs={{0,6},{2,0},{4,2},{6,4},{1,7},{3,1},{5,3},{7,5},{8,14},{10,8},{12,... | collective-permute-start | bytes 3145736 | tf_op jit(solution)/shard_map/ppermute | solution.py:449
  144.0 1.5 collective-permute-start.25
  145.5 10.4 %output.3 = (bf16[64,8192]{1,0:T(8,128)(2,1)S(1)}, bf16[64,8192]{1,0:T(8,128)(2,1)S(1)}, bf16[64,8192]{1,0:T(8,128)(2,1)S(1)}, bf16[32,8192]{1,0:T(8,128)(2,1)S(1)}, bf16[32,8192]{1,0:T(8,128)(2,1)S(1)}) custom-call(bf16[512,1024]{1,0:T(8,128)(2,1)S(1)} %get-tuple-element.133.mixed_ref, bf16[512,8192]{1,0:T(8,128)(2,1)} %mine_ref.1, ...), custom_call_target="tpu_custom_call" | custom-call | flops 4294967296 | bytes 20971520 | tf_op jit(solution)/shard_map/output/pallas_call | solution.py:272
  156.0 3.2 %collective-permute-start.31 = (bf16[32,8192]{1,0:T(8,128)(2,1)S(1)}, bf16[32,8192]{1,0:T(8,128)(2,1)S(1)}, u32[]{:S(2)}, u32[]{:S(2)}) collective-permute-start(bf16[32,8192]{1,0:T(8,128)(2,1)S(1)} %get-tuple-element.152), channel_id=1, source_target_pairs={{0,6},{2,0},{4,2},{6,4},{1,7},{3,1},{5,3},{7,5},{8,14},{10,8},{12,... | collective-permute-start | bytes 1572872 | tf_op jit(solution)/shard_map/ppermute | solution.py:449
  159.2 1.8 collective-permute-start.26
  161.0 4.6 %collective-permute-done.26.refs_1_ = bf16[1024,128]{1,0:T(8,128)(2,1)S(1)} collective-permute-done((bf16[1024,128]{1,0:T(8,128)(2,1)S(1)}, bf16[1024,128]{1,0:T(8,128)(2,1)S(1)}, u32[]{:S(2)}, u32[]{:S(2)}) %collective-permute-start.26) | collective-permute-done | bytes 262176 | tf_op jit(solution)/shard_map/ppermute | solution.py:449
  165.6 2.5 %collective-permute-done.23.refs_1_ = bf16[64,8192]{1,0:T(8,128)(2,1)S(1)} collective-permute-done((bf16[64,8192]{1,0:T(8,128)(2,1)S(1)}, bf16[64,8192]{1,0:T(8,128)(2,1)S(1)}, u32[]{:S(2)}, u32[]{:S(2)}) %collective-permute-start.23) | collective-permute-done | bytes 1048608 | tf_op jit(solution)/shard_map/ppermute | solution.py:449
  168.1 0.4 split.1
  168.8 3.0 %collective-permute-start.28 = (bf16[32,8192]{1,0:T(8,128)(2,1)S(1)}, bf16[32,8192]{1,0:T(8,128)(2,1)S(1)}, u32[]{:S(2)}, u32[]{:S(2)}) collective-permute-start(bf16[32,8192]{1,0:T(8,128)(2,1)S(1)} %get-tuple-element.146), channel_id=1, source_target_pairs={{0,24},{16,0},{8,16},{24,8},{1,25},{17,1},{9,17},{25,9},{2,26},{18... | collective-permute-start | bytes 1572872 | tf_op jit(solution)/shard_map/ppermute | solution.py:449
  171.8 4.2 %collective-permute-done.30.refs_1_ = bf16[32,8192]{1,0:T(8,128)(2,1)S(1)} collective-permute-done((bf16[32,8192]{1,0:T(8,128)(2,1)S(1)}, bf16[32,8192]{1,0:T(8,128)(2,1)S(1)}, u32[]{:S(2)}, u32[]{:S(2)}) %collective-permute-start.30) | collective-permute-done | bytes 524320 | tf_op jit(solution)/shard_map/ppermute | solution.py:449
  176.5 3.0 %collective-permute-start.33 = (bf16[64,8192]{1,0:T(8,128)(2,1)S(1)}, bf16[64,8192]{1,0:T(8,128)(2,1)S(1)}, u32[]{:S(2)}, u32[]{:S(2)}) collective-permute-start(bf16[64,8192]{1,0:T(8,128)(2,1)S(1)} %get-tuple-element.154), channel_id=1, source_target_pairs={{0,6},{2,0},{4,2},{6,4},{1,7},{3,1},{5,3},{7,5},{8,14},{10,8},{12,... | collective-permute-start | bytes 3145736 | tf_op jit(solution)/shard_map/ppermute | solution.py:449
  179.6 1.5 collective-permute-start.29
  181.0 6.1 %collective-permute-done.29.refs_3_ = bf16[1024,128]{1,0:T(8,128)(2,1)S(1)} collective-permute-done((bf16[1024,128]{1,0:T(8,128)(2,1)S(1)}, bf16[1024,128]{1,0:T(8,128)(2,1)S(1)}, u32[]{:S(2)}, u32[]{:S(2)}) %collective-permute-start.29) | collective-permute-done | bytes 262176 | tf_op jit(solution)/shard_map/ppermute | solution.py:449
  187.2 0.6 collective-permute-start.34
  187.8 2.6 %collective-permute-start.35 = (bf16[32,8192]{1,0:T(8,128)(2,1)S(1)}, bf16[32,8192]{1,0:T(8,128)(2,1)S(1)}, u32[]{:S(2)}, u32[]{:S(2)}) collective-permute-start(bf16[32,8192]{1,0:T(8,128)(2,1)S(1)} %collective-permute-done.28), channel_id=1, source_target_pairs={{0,24},{16,0},{8,16},{24,8},{1,25},{17,1},{9,17},{25,9},{2,26},{18... | collective-permute-start | bytes 1572872 | tf_op jit(solution)/shard_map/ppermute | solution.py:449
  190.4 1.8 apply.1
  192.2 7.1 %collective-permute-done.32.refs_1_ = bf16[64,8192]{1,0:T(8,128)(2,1)S(1)} collective-permute-done((bf16[64,8192]{1,0:T(8,128)(2,1)S(1)}, bf16[64,8192]{1,0:T(8,128)(2,1)S(1)}, u32[]{:S(2)}, u32[]{:S(2)}) %collective-permute-start.32) | collective-permute-done | bytes 1048608 | tf_op jit(solution)/shard_map/ppermute | solution.py:449
  199.4 1.5 finish.1
  (72 shorter events, 2.7 us)
Async XLA Ops:
  0.6 1.2 copy-start.9
  1.9 0.8 copy-start.17
  4.2 28.1 %copy-start.6 = (bf16[64,8192]{1,0:T(8,128)(2,1)}, bf16[64,8192]{1,0:T(8,128)(2,1)S(1)}, u32[]{:S(2)}) copy-start(bf16[64,8192]{1,0:T(8,128)(2,1)S(1)} %get-tuple-element.83.refs_0_) | copy-start | bytes 3145732
  4.2 19.8 %collective-permute-start.2 = (bf16[8192,128]{1,0:T(8,128)(2,1)}, bf16[8192,128]{1,0:T(8,128)(2,1)S(1)}, u32[]{:S(2)}, u32[]{:S(2)}) collective-permute-start(bf16[8192,128]{1,0:T(8,128)(2,1)} %refs_4_.5), channel_id=1, source_target_pairs={{0,1},{1,0},{2,3},{3,2},{4,5},{5,4},{6,7},{7,6},{8,9},{9,8},{10,11... | collective-permute-start | bytes 6291464 | tf_op jit(solution)/shard_map/ppermute | solution.py:444
  4.2 28.1 %collective-permute-start.5 = (bf16[64,8192]{1,0:T(8,128)(2,1)S(1)}, bf16[64,8192]{1,0:T(8,128)(2,1)}, u32[]{:S(2)}, u32[]{:S(2)}) collective-permute-start(bf16[64,8192]{1,0:T(8,128)(2,1)S(1)} %get-tuple-element.83.refs_0_), channel_id=1, source_target_pairs={{0,2},{2,4},{4,6},{6,0},{1,3},{3,5},{5,7},{7,1},{8,10},{10,12},{12... | collective-permute-start | bytes 3145736 | tf_op jit(solution)/shard_map/ppermute | solution.py:449
  6.2 26.1 %collective-permute-start.6 = (bf16[64,8192]{1,0:T(8,128)(2,1)S(1)}, bf16[64,8192]{1,0:T(8,128)(2,1)}, u32[]{:S(2)}, u32[]{:S(2)}) collective-permute-start(bf16[64,8192]{1,0:T(8,128)(2,1)S(1)} %get-tuple-element.83.refs_0_), channel_id=1, source_target_pairs={{0,6},{2,0},{4,2},{6,4},{1,7},{3,1},{5,3},{7,5},{8,14},{10,8},{12,... | collective-permute-start | bytes 3145736 | tf_op jit(solution)/shard_map/ppermute | solution.py:449
  8.4 15.6 %collective-permute-start = (bf16[32,8192]{1,0:T(8,128)(2,1)}, bf16[32,8192]{1,0:T(8,128)(2,1)}, u32[]{:S(2)}, u32[]{:S(2)}) collective-permute-start(bf16[32,8192]{1,0:T(8,128)(2,1)} %get-tuple-element.81), channel_id=1, source_target_pairs={{0,16},{16,8},{8,24},{24,0},{1,17},{17,9},{9,25},{25,1},{2,18},{18... | collective-permute-start | bytes 1572872 | tf_op jit(solution)/shard_map/ppermute | solution.py:449
  10.0 14.0 %collective-permute-start.1 = (bf16[32,8192]{1,0:T(8,128)(2,1)}, bf16[32,8192]{1,0:T(8,128)(2,1)}, u32[]{:S(2)}, u32[]{:S(2)}) collective-permute-start(bf16[32,8192]{1,0:T(8,128)(2,1)} %get-tuple-element.82), channel_id=1, source_target_pairs={{0,24},{16,0},{8,16},{24,8},{1,25},{17,1},{9,17},{25,9},{2,26},{18... | collective-permute-start | bytes 1572872 | tf_op jit(solution)/shard_map/ppermute | solution.py:449
  12.6 1.2 copy-start.8
  15.7 0.7 copy-start.11
  16.4 0.7 copy-start.16
  17.1 0.7 copy-start.18
  24.0 1.3 copy-start.3
  25.4 13.7 %collective-permute-start.4 = (bf16[32,8192]{1,0:T(8,128)(2,1)}, bf16[32,8192]{1,0:T(8,128)(2,1)S(1)}, u32[]{:S(2)}, u32[]{:S(2)}) collective-permute-start(bf16[32,8192]{1,0:T(8,128)(2,1)} %collective-permute-done.1), channel_id=1, source_target_pairs={{0,24},{16,0},{8,16},{24,8},{1,25},{17,1},{9,17},{25,9},{2,26},{18... | collective-permute-start | bytes 1572872 | tf_op jit(solution)/shard_map/ppermute | solution.py:449
  28.3 14.0 %collective-permute-start.3 = (bf16[32,8192]{1,0:T(8,128)(2,1)}, bf16[32,8192]{1,0:T(8,128)(2,1)S(1)}, u32[]{:S(2)}, u32[]{:S(2)}) collective-permute-start(bf16[32,8192]{1,0:T(8,128)(2,1)} %collective-permute-done), channel_id=1, source_target_pairs={{0,16},{16,8},{8,24},{24,0},{1,17},{17,9},{9,25},{25,1},{2,18},{18... | collective-permute-start | bytes 1572872 | tf_op jit(solution)/shard_map/ppermute | solution.py:449
  28.3 18.9 %collective-permute-start.9 = (bf16[8192,512]{1,0:T(8,128)(2,1)}, bf16[8192,512]{1,0:T(8,128)(2,1)}, u32[]{:S(2)}, u32[]{:S(2)}) collective-permute-start(bf16[8192,512]{1,0:T(8,128)(2,1)} %refs_2_.1), channel_id=1, source_target_pairs={{0,1},{1,0},{2,3},{3,2},{4,5},{5,4},{6,7},{7,6},{8,9},{9,8},{10,11... | collective-permute-start | bytes 25165832 | tf_op jit(solution)/shard_map/ppermute | solution.py:444
  32.3 14.9 %copy-start.2 = (bf16[8192,128]{1,0:T(8,128)(2,1)S(1)}, bf16[8192,128]{1,0:T(8,128)(2,1)}, u32[]{:S(2)}) copy-start(bf16[8192,128]{1,0:T(8,128)(2,1)} %refs_4_.5) | copy-start | bytes 6291460
  32.3 32.4 %collective-permute-start.8 = (bf16[64,8192]{1,0:T(8,128)(2,1)}, bf16[64,8192]{1,0:T(8,128)(2,1)}, u32[]{:S(2)}, u32[]{:S(2)}) collective-permute-start(bf16[64,8192]{1,0:T(8,128)(2,1)} %get-tuple-element.96.refs_2_), channel_id=1, source_target_pairs={{0,2},{2,4},{4,6},{6,0},{1,3},{3,5},{5,7},{7,1},{8,10},{10,12},{12... | collective-permute-start | bytes 3145736 | tf_op jit(solution)/shard_map/ppermute | solution.py:449
  42.4 23.2 %collective-permute-start.7 = (bf16[64,8192]{1,0:T(8,128)(2,1)S(1)}, bf16[64,8192]{1,0:T(8,128)(2,1)}, u32[]{:S(2)}, u32[]{:S(2)}) collective-permute-start(bf16[64,8192]{1,0:T(8,128)(2,1)S(1)} %pad_maximum_fusion.refs_3_), channel_id=1, source_target_pairs={{0,6},{2,0},{4,2},{6,4},{1,7},{3,1},{5,3},{7,5},{8,14},{10,8},{12,... | collective-permute-start | bytes 3145736 | tf_op jit(solution)/shard_map/ppermute | solution.py:449
  44.0 20.8 %collective-permute-start.10 = (bf16[1024,128]{1,0:T(8,128)(2,1)}, bf16[1024,128]{1,0:T(8,128)(2,1)S(1)}, u32[]{:S(2)}, u32[]{:S(2)}) collective-permute-start(bf16[1024,128]{1,0:T(8,128)(2,1)} %get-tuple-element.103), channel_id=1, source_target_pairs={{0,32},{32,64},{64,96},{96,0},{1,33},{33,65},{65,97},{97,1},{2,34}... | collective-permute-start | bytes 786440 | tf_op jit(solution)/shard_map/ppermute | solution.py:449
  45.5 19.3 %collective-permute-start.11 = (bf16[1024,128]{1,0:T(8,128)(2,1)}, bf16[1024,128]{1,0:T(8,128)(2,1)S(1)}, u32[]{:S(2)}, u32[]{:S(2)}) collective-permute-start(bf16[1024,128]{1,0:T(8,128)(2,1)} %copy-done.18), channel_id=1, source_target_pairs={{0,96},{32,0},{64,32},{96,64},{1,97},{33,1},{65,33},{97,65},{2,98}... | collective-permute-start | bytes 786440 | tf_op jit(solution)/shard_map/ppermute | solution.py:449
  47.2 3.4 %copy-start = (bf16[8192,512]{1,0:T(8,128)(2,1)S(1)}, bf16[8192,512]{1,0:T(8,128)(2,1)}, u32[]{:S(2)}) copy-start(bf16[8192,512]{1,0:T(8,128)(2,1)} %refs_2_.1) | copy-start | bytes 25165828
  50.6 1.6 copy-start.4
  52.2 1.2 copy-start.7
  63.9 0.8 copy-start.13
  64.7 0.9 copy-start.19
  65.6 36.3 %collective-permute-start.18 = (bf16[512,8192]{1,0:T(8,128)(2,1)}, bf16[512,8192]{1,0:T(8,128)(2,1)}, u32[]{:S(2)}, u32[]{:S(2)}) collective-permute-start(bf16[512,8192]{1,0:T(8,128)(2,1)} %mine_ref.1), channel_id=1, source_target_pairs={{0,1},{1,0},{2,3},{3,2},{4,5},{5,4},{6,7},{7,6},{8,9},{9,8},{10,11... | collective-permute-start | bytes 25165832 | tf_op jit(solution)/shard_map/ppermute | solution.py:444
  65.6 26.9 %collective-permute-start.12 = (bf16[64,8192]{1,0:T(8,128)(2,1)S(1)}, bf16[64,8192]{1,0:T(8,128)(2,1)}, u32[]{:S(2)}, u32[]{:S(2)}) collective-permute-start(bf16[64,8192]{1,0:T(8,128)(2,1)S(1)} %pad_maximum_fusion.refs_3_), channel_id=1, source_target_pairs={{0,2},{2,4},{4,6},{6,0},{1,3},{3,5},{5,7},{7,1},{8,10},{10,12},{12... | collective-permute-start | bytes 3145736 | tf_op jit(solution)/shard_map/ppermute | solution.py:449
  65.6 26.9 %collective-permute-start.13 = (bf16[64,8192]{1,0:T(8,128)(2,1)}, bf16[64,8192]{1,0:T(8,128)(2,1)}, u32[]{:S(2)}, u32[]{:S(2)}) collective-permute-start(bf16[64,8192]{1,0:T(8,128)(2,1)} %collective-permute-done.7.refs_1_), channel_id=1, source_target_pairs={{0,6},{2,0},{4,2},{6,4},{1,7},{3,1},{5,3},{7,5},{8,14},{10,8},{12,... | collective-permute-start | bytes 3145736 | tf_op jit(solution)/shard_map/ppermute | solution.py:449
  70.7 21.9 %collective-permute-start.14 = (bf16[1024,128]{1,0:T(8,128)(2,1)}, bf16[1024,128]{1,0:T(8,128)(2,1)}, u32[]{:S(2)}, u32[]{:S(2)}) collective-permute-start(bf16[1024,128]{1,0:T(8,128)(2,1)} %add_convert_fusion), channel_id=1, source_target_pairs={{0,32},{32,64},{64,96},{96,0},{1,33},{33,65},{65,97},{97,1},{2,34}... | collective-permute-start | bytes 786440 | tf_op jit(solution)/shard_map/ppermute | solution.py:449
  72.3 29.6 %collective-permute-start.15 = (bf16[256,256]{1,0:T(8,128)(2,1)S(1)}, bf16[256,256]{1,0:T(8,128)(2,1)S(1)}, u32[]{:S(2)}, u32[]{:S(2)}) collective-permute-start(bf16[256,256]{1,0:T(8,128)(2,1)S(1)} %get-tuple-element.116.refs_3_), channel_id=1, source_target_pairs={{0,1},{1,0},{2,3},{3,2},{4,5},{5,4},{6,7},{7,6},{8,9},{9,8},{10,11... | collective-permute-start | bytes 393224 | tf_op jit(solution)/shard_map/ppermute | solution.py:444
  72.5 3.4 %copy-start.1 = (bf16[8192,512]{1,0:T(8,128)(2,1)S(1)}, bf16[8192,512]{1,0:T(8,128)(2,1)}, u32[]{:S(2)}) copy-start(bf16[8192,512]{1,0:T(8,128)(2,1)} %refs_2_.1) | copy-start | bytes 25165828
  75.9 1.6 copy-start.5
  92.5 9.4 %collective-permute-start.16 = (bf16[128,256]{1,0:T(8,128)(2,1)S(1)}, bf16[128,256]{1,0:T(8,128)(2,1)S(1)}, u32[]{:S(2)}, u32[]{:S(2)}) collective-permute-start(bf16[128,256]{1,0:T(8,128)(2,1)S(1)} %get-tuple-element.117.refs_4_), channel_id=1, source_target_pairs={{0,1},{1,0},{2,3},{3,2},{4,5},{5,4},{6,7},{7,6},{8,9},{9,8},{10,11... | collective-permute-start | bytes 196616 | tf_op jit(solution)/shard_map/ppermute | solution.py:444
  92.5 8.4 %copy-start.12 = (bf16[1024,128]{1,0:T(8,128)(2,1)S(1)}, bf16[1024,128]{1,0:T(8,128)(2,1)}, u32[]{:S(2)}) copy-start(bf16[1024,128]{1,0:T(8,128)(2,1)} %copy-done.11) | copy-start | bytes 786436
  92.5 9.4 %copy-start.14 = (bf16[256,1024]{1,0:T(8,128)(2,1)S(1)}, bf16[256,1024]{1,0:T(8,128)(2,1)}, u32[]{:S(2)}) copy-start(bf16[256,1024]{1,0:T(8,128)(2,1)} %copy-done.13) | copy-start | bytes 1572868
  100.4 1.6 collective-permute-start.17
  114.3 26.1 %collective-permute-start.19 = (bf16[32,8192]{1,0:T(8,128)(2,1)S(1)}, bf16[32,8192]{1,0:T(8,128)(2,1)S(1)}, u32[]{:S(2)}, u32[]{:S(2)}) collective-permute-start(bf16[32,8192]{1,0:T(8,128)(2,1)S(1)} %get-tuple-element.122), channel_id=1, source_target_pairs={{0,2},{2,4},{4,6},{6,0},{1,3},{3,5},{5,7},{7,1},{8,10},{10,12},{12... | collective-permute-start | bytes 1572872 | tf_op jit(solution)/shard_map/ppermute | solution.py:449
  114.8 25.6 %collective-permute-start.20 = (bf16[32,8192]{1,0:T(8,128)(2,1)S(1)}, bf16[32,8192]{1,0:T(8,128)(2,1)S(1)}, u32[]{:S(2)}, u32[]{:S(2)}) collective-permute-start(bf16[32,8192]{1,0:T(8,128)(2,1)S(1)} %get-tuple-element.124), channel_id=1, source_target_pairs={{0,6},{2,0},{4,2},{6,4},{1,7},{3,1},{5,3},{7,5},{8,14},{10,8},{12,... | collective-permute-start | bytes 1572872 | tf_op jit(solution)/shard_map/ppermute | solution.py:449
  117.6 15.3 %copy-start.15 = (f32[512,128]{1,0:T(8,128)S(1)}, f32[512,128]{1,0:T(8,128)}, u32[]{:S(2)}) copy-start(f32[512,128]{1,0:T(8,128)} %refs_4_.6) | copy-start | bytes 786436
  127.5 5.4 %collective-permute-start.21 = (bf16[512,128]{1,0:T(8,128)(2,1)S(1)}, bf16[512,128]{1,0:T(8,128)(2,1)S(1)}, u32[]{:S(2)}, u32[]{:S(2)}) collective-permute-start(bf16[512,128]{1,0:T(8,128)(2,1)S(1)} %add_convert_fusion.1), channel_id=1, source_target_pairs={{0,16},{16,0},{1,17},{17,1},{2,18},{18,2},{3,19},{19,3},{4,20},{20... | collective-permute-start | bytes 393224 | tf_op jit(solution)/shard_map/ppermute | solution.py:444
  135.3 5.0 %collective-permute-start.22 = (bf16[512,128]{1,0:T(8,128)(2,1)S(1)}, bf16[512,128]{1,0:T(8,128)(2,1)S(1)}, u32[]{:S(2)}, u32[]{:S(2)}) collective-permute-start(bf16[512,128]{1,0:T(8,128)(2,1)S(1)} %get-tuple-element.132), channel_id=1, source_target_pairs={{0,16},{16,0},{1,17},{17,1},{2,18},{18,2},{3,19},{19,3},{4,20},{20... | collective-permute-start | bytes 393224 | tf_op jit(solution)/shard_map/ppermute | solution.py:444
  140.7 27.4 %collective-permute-start.23 = (bf16[64,8192]{1,0:T(8,128)(2,1)S(1)}, bf16[64,8192]{1,0:T(8,128)(2,1)S(1)}, u32[]{:S(2)}, u32[]{:S(2)}) collective-permute-start(bf16[64,8192]{1,0:T(8,128)(2,1)S(1)} %get-tuple-element.136), channel_id=1, source_target_pairs={{0,2},{2,4},{4,6},{6,0},{1,3},{3,5},{5,7},{7,1},{8,10},{10,12},{12... | collective-permute-start | bytes 3145736 | tf_op jit(solution)/shard_map/ppermute | solution.py:449
  140.8 27.3 %collective-permute-start.24 = (bf16[64,8192]{1,0:T(8,128)(2,1)S(1)}, bf16[64,8192]{1,0:T(8,128)(2,1)S(1)}, u32[]{:S(2)}, u32[]{:S(2)}) collective-permute-start(bf16[64,8192]{1,0:T(8,128)(2,1)S(1)} %get-tuple-element.137), channel_id=1, source_target_pairs={{0,6},{2,0},{4,2},{6,4},{1,7},{3,1},{5,3},{7,5},{8,14},{10,8},{12,... | collective-permute-start | bytes 3145736 | tf_op jit(solution)/shard_map/ppermute | solution.py:449
  144.0 15.2 %collective-permute-start.25 = (bf16[1024,128]{1,0:T(8,128)(2,1)S(1)}, bf16[1024,128]{1,0:T(8,128)(2,1)S(1)}, u32[]{:S(2)}, u32[]{:S(2)}) collective-permute-start(bf16[1024,128]{1,0:T(8,128)(2,1)S(1)} %pad_maximum_fusion.1.refs_0_), channel_id=1, source_target_pairs={{0,32},{32,64},{64,96},{96,0},{1,33},{33,65},{65,97},{97,1},{2,34}... | collective-permute-start | bytes 786440 | tf_op jit(solution)/shard_map/ppermute | solution.py:449
  155.9 20.1 %collective-permute-start.30 = (bf16[32,8192]{1,0:T(8,128)(2,1)S(1)}, bf16[32,8192]{1,0:T(8,128)(2,1)S(1)}, u32[]{:S(2)}, u32[]{:S(2)}) collective-permute-start(bf16[32,8192]{1,0:T(8,128)(2,1)S(1)} %get-tuple-element.150), channel_id=1, source_target_pairs={{0,2},{2,4},{4,6},{6,0},{1,3},{3,5},{5,7},{7,1},{8,10},{10,12},{12... | collective-permute-start | bytes 1572872 | tf_op jit(solution)/shard_map/ppermute | solution.py:449
  156.0 20.0 %collective-permute-start.31 = (bf16[32,8192]{1,0:T(8,128)(2,1)S(1)}, bf16[32,8192]{1,0:T(8,128)(2,1)S(1)}, u32[]{:S(2)}, u32[]{:S(2)}) collective-permute-start(bf16[32,8192]{1,0:T(8,128)(2,1)S(1)} %get-tuple-element.152), channel_id=1, source_target_pairs={{0,6},{2,0},{4,2},{6,4},{1,7},{3,1},{5,3},{7,5},{8,14},{10,8},{12,... | collective-permute-start | bytes 1572872 | tf_op jit(solution)/shard_map/ppermute | solution.py:449
  159.2 6.4 %collective-permute-start.26 = (bf16[1024,128]{1,0:T(8,128)(2,1)S(1)}, bf16[1024,128]{1,0:T(8,128)(2,1)S(1)}, u32[]{:S(2)}, u32[]{:S(2)}) collective-permute-start(bf16[1024,128]{1,0:T(8,128)(2,1)S(1)} %pad_maximum_fusion.1.refs_0_), channel_id=1, source_target_pairs={{0,96},{32,0},{64,32},{96,64},{1,97},{33,1},{65,33},{97,65},{2,98}... | collective-permute-start | bytes 786440 | tf_op jit(solution)/shard_map/ppermute | solution.py:449
  168.5 21.9 %copy-start.10 = (bf16[512,1024]{1,0:T(8,128)(2,1)S(1)}, bf16[512,1024]{1,0:T(8,128)(2,1)}, u32[]{:S(2)}) copy-start(bf16[512,1024]{1,0:T(8,128)(2,1)} %params_ref.1) | copy-start | bytes 3145732
  168.5 18.7 %collective-permute-start.27 = (bf16[32,8192]{1,0:T(8,128)(2,1)S(1)}, bf16[32,8192]{1,0:T(8,128)(2,1)S(1)}, u32[]{:S(2)}, u32[]{:S(2)}) collective-permute-start(bf16[32,8192]{1,0:T(8,128)(2,1)S(1)} %get-tuple-element.145), channel_id=1, source_target_pairs={{0,16},{16,8},{8,24},{24,0},{1,17},{17,9},{9,25},{25,1},{2,18},{18... | collective-permute-start | bytes 1572872 | tf_op jit(solution)/shard_map/ppermute | solution.py:449
  168.8 18.3 %collective-permute-start.28 = (bf16[32,8192]{1,0:T(8,128)(2,1)S(1)}, bf16[32,8192]{1,0:T(8,128)(2,1)S(1)}, u32[]{:S(2)}, u32[]{:S(2)}) collective-permute-start(bf16[32,8192]{1,0:T(8,128)(2,1)S(1)} %get-tuple-element.146), channel_id=1, source_target_pairs={{0,24},{16,0},{8,16},{24,8},{1,25},{17,1},{9,17},{25,9},{2,26},{18... | collective-permute-start | bytes 1572872 | tf_op jit(solution)/shard_map/ppermute | solution.py:449
  176.3 23.1 %collective-permute-start.32 = (bf16[64,8192]{1,0:T(8,128)(2,1)S(1)}, bf16[64,8192]{1,0:T(8,128)(2,1)S(1)}, u32[]{:S(2)}, u32[]{:S(2)}) collective-permute-start(bf16[64,8192]{1,0:T(8,128)(2,1)S(1)} %get-tuple-element.153), channel_id=1, source_target_pairs={{0,2},{2,4},{4,6},{6,0},{1,3},{3,5},{5,7},{7,1},{8,10},{10,12},{12... | collective-permute-start | bytes 3145736 | tf_op jit(solution)/shard_map/ppermute | solution.py:449
  176.5 22.8 %collective-permute-start.33 = (bf16[64,8192]{1,0:T(8,128)(2,1)S(1)}, bf16[64,8192]{1,0:T(8,128)(2,1)S(1)}, u32[]{:S(2)}, u32[]{:S(2)}) collective-permute-start(bf16[64,8192]{1,0:T(8,128)(2,1)S(1)} %get-tuple-element.154), channel_id=1, source_target_pairs={{0,6},{2,0},{4,2},{6,4},{1,7},{3,1},{5,3},{7,5},{8,14},{10,8},{12,... | collective-permute-start | bytes 3145736 | tf_op jit(solution)/shard_map/ppermute | solution.py:449
  179.6 7.6 %collective-permute-start.29 = (bf16[1024,128]{1,0:T(8,128)(2,1)S(1)}, bf16[1024,128]{1,0:T(8,128)(2,1)S(1)}, u32[]{:S(2)}, u32[]{:S(2)}) collective-permute-start(bf16[1024,128]{1,0:T(8,128)(2,1)S(1)} %collective-permute-done.25.refs_2_), channel_id=1, source_target_pairs={{0,32},{32,64},{64,96},{96,0},{1,33},{33,65},{65,97},{97,1},{2,34}... | collective-permute-start | bytes 786440 | tf_op jit(solution)/shard_map/ppermute | solution.py:449
  187.2 12.2 %collective-permute-start.34 = (bf16[32,8192]{1,0:T(8,128)(2,1)S(1)}, bf16[32,8192]{1,0:T(8,128)(2,1)S(1)}, u32[]{:S(2)}, u32[]{:S(2)}) collective-permute-start(bf16[32,8192]{1,0:T(8,128)(2,1)S(1)} %collective-permute-done.27), channel_id=1, source_target_pairs={{0,16},{16,8},{8,24},{24,0},{1,17},{17,9},{9,25},{25,1},{2,18},{18... | collective-permute-start | bytes 1572872 | tf_op jit(solution)/shard_map/ppermute | solution.py:449
  187.8 11.6 %collective-permute-start.35 = (bf16[32,8192]{1,0:T(8,128)(2,1)S(1)}, bf16[32,8192]{1,0:T(8,128)(2,1)S(1)}, u32[]{:S(2)}, u32[]{:S(2)}) collective-permute-start(bf16[32,8192]{1,0:T(8,128)(2,1)S(1)} %collective-permute-done.28), channel_id=1, source_target_pairs={{0,24},{16,0},{8,16},{24,8},{1,25},{17,1},{9,17},{25,9},{2,26},{18... | collective-permute-start | bytes 1572872 | tf_op jit(solution)/shard_map/ppermute | solution.py:449
